TPU v7x, 256 devices: a whole 4x4x8 slice. The times are simulated.
256 devices in a mesh: tile: 32 (over x, z), band: 8 (over y, core).
Axes of the slice: x: 4, y: 4, z: 8, core: 2. Of those that a mesh axis runs over, the one named last changes fastest.
Arguments:
- traces: bfloat16 [65536, 1024], P('tile', 'band'), may hold values from -6 to 6
- route: int32 [65536, 1], P('tile'), may hold values from 0 to 31; in each aligned block of 2048 rows (0 to 2047, 2048 to 4095, ...) at most 128 rows name the same one
- mid_x: int32 [65536], P('tile'), may hold values from 0 to 255
- mid_y: int32 [65536], P('tile'), may hold values from 0 to 255
- band_low: int32 [32], P('tile'), may hold values from 0 to 7
- band_high: int32 [32], P('tile'), may hold values from 25 to 32
- offset_bin: int32 [32], P('tile'), may hold values from 0 to 7
- azimuth_bin: int32 [32], P('tile'), may hold values from 0 to 11
Outputs:
- amo_out: float32 [32, 32, 256, 512], P('tile', 'band')
Inputs may be any that keep to these rules, and one draw needn't show every extreme that they name: `route`: within each aligned block of 2048 traces (one shot shard) no tile is named more than 128 times, a bound that some block reaches.
All inputs are finite; a program needn't handle non-finite values.
Results may differ from a plain program's by a relative error of at most 0.009.
Values may be sent and summed in bfloat16 or wider, within the bound.
No kernel may reach another device: no remote copies, remote signals or barrier semaphores. Data moves between devices by JAX's collectives and lax.ppermute only.
A program may use at most 64 MiB of HBM per device.

v0:
```python
import math

import jax
import jax.numpy as jnp
from jax import lax
from jax.sharding import PartitionSpec as P

MIDS = 256
AZIMUTHS = 12
F_DEV = 4


LOG_ANCHOR = 64.0


def log_omegas(first_index, freq_count, trace_length):
    log_span = math.log((trace_length + LOG_ANCHOR) / LOG_ANCHOR)
    steps_up = jnp.arange(freq_count, dtype=jnp.int32) + first_index + 1
    return steps_up.astype(jnp.float32) * (2.0 * math.pi / log_span)


def time_kernel(sample_count, trace_length, freq_count):
    samples = jnp.arange(sample_count, dtype=jnp.int32).astype(jnp.float32)
    stretch = jnp.log((samples + LOG_ANCHOR) / LOG_ANCHOR)
    omegas = log_omegas(0, freq_count, trace_length)
    angles = stretch[:, None] * omegas[None, :]
    weight = trace_length ** (-0.5)
    stacked = jnp.stack([jnp.cos(angles) * weight, -jnp.sin(angles) * weight], axis=2)
    return stacked.reshape(sample_count, 2 * freq_count).astype(jnp.bfloat16)


def forward_rows(positions, grid_size):
    wave_index = jnp.arange(grid_size, dtype=jnp.int32)
    phase_turns = positions[:, None] * wave_index[None, :] % grid_size
    angles = phase_turns.astype(jnp.float32) * (2.0 * math.pi / grid_size)
    return (jnp.cos(angles), -jnp.sin(angles))


def inverse_blocks(grid_size):
    wave_index = jnp.arange(grid_size, dtype=jnp.int32)
    phase_turns = wave_index[:, None] * wave_index[None, :] % grid_size
    angles = phase_turns.astype(jnp.float32) * (2.0 * math.pi / grid_size)
    cosine_table = jnp.cos(angles)
    sine_table = jnp.sin(angles)
    left_side = jnp.concatenate(
        [
            jnp.concatenate([cosine_table, -sine_table], axis=1),
            jnp.concatenate([sine_table, cosine_table], axis=1),
        ],
        axis=0,
    )
    right_side = jnp.concatenate(
        [
            jnp.concatenate([cosine_table, sine_table], axis=1),
            jnp.concatenate([-sine_table, cosine_table], axis=1),
        ],
        axis=0,
    )
    return (left_side.astype(jnp.bfloat16), right_side.astype(jnp.bfloat16))


def accumulate(spectra, pos_x, pos_y, grid_size, weight):
    row_total = spectra.shape[0]
    freq_count = spectra.shape[1] // 2
    row_block = math.gcd(row_total, 512)

    def add_rows(step_number, running):
        start_row = step_number * row_block
        spectra_rows = lax.dynamic_slice_in_dim(spectra, start_row, row_block, 0)
        spectra_rows = spectra_rows.astype(jnp.float32).reshape(row_block, freq_count, 2)
        block_x = lax.dynamic_slice_in_dim(pos_x, start_row, row_block, 0)
        block_y = lax.dynamic_slice_in_dim(pos_y, start_row, row_block, 0)
        cosine_x, sine_x = forward_rows(block_x, grid_size)
        cosine_y, sine_y = forward_rows(block_y, grid_size)
        real_part = spectra_rows[:, :, 0:1] * weight
        imag_part = spectra_rows[:, :, 1:2] * weight
        left_real = real_part * cosine_x[:, None, :] - imag_part * sine_x[:, None, :]
        left_imag = real_part * sine_x[:, None, :] + imag_part * cosine_x[:, None, :]
        left_rows = jnp.concatenate([left_real, left_imag], axis=2).astype(jnp.bfloat16)
        left_rows = left_rows.reshape(row_block, freq_count * 2 * grid_size)
        right_rows = jnp.concatenate([cosine_y, sine_y], axis=1).astype(jnp.bfloat16)
        return running + lax.dot_general(
            left_rows, right_rows, (((0,), (0,)), ((), ())), preferred_element_type=jnp.float32
        )

    running = jnp.zeros((freq_count * 2 * grid_size, 2 * grid_size), jnp.float32)
    running = lax.fori_loop(0, row_total // row_block, add_rows, running)
    running = running.reshape(freq_count, 2, grid_size, 2, grid_size)
    real_part = running[:, 0, :, 0, :] - running[:, 1, :, 1, :]
    imag_part = running[:, 0, :, 1, :] + running[:, 1, :, 0, :]
    return (real_part, imag_part)


def amo_phase(omegas, offset_value, azimuth_value, grid_size):
    wave_index = jnp.arange(grid_size, dtype=jnp.int32)
    signed = jnp.where(wave_index >= grid_size // 2, wave_index - grid_size, wave_index)
    wavenumber = signed.astype(jnp.float32) * (2.0 * math.pi / grid_size)
    offset_length = (offset_value.astype(jnp.float32) + 1.0) * 0.5
    azimuth_angle = azimuth_value.astype(jnp.float32) * (math.pi / AZIMUTHS)
    inline = wavenumber[:, None] * (offset_length * jnp.cos(azimuth_angle)) + wavenumber[
        None, :
    ] * (offset_length * jnp.sin(azimuth_angle))
    along_target = wavenumber[:, None] * offset_length + jnp.zeros((1, grid_size), jnp.float32)
    change = jnp.log1p(along_target * along_target) - jnp.log1p(inline * inline)
    return 0.5 * omegas[:, None, None] * change[None, :, :]


def finish(real_part, imag_part, phase_table, live_mask, grid_size):
    cosine_phase = jnp.cos(phase_table)
    sine_phase = jnp.sin(phase_table)
    moved_real = (real_part * cosine_phase - imag_part * sine_phase) * live_mask[:, None, None]
    moved_imag = (real_part * sine_phase + imag_part * cosine_phase) * live_mask[:, None, None]
    stacked = jnp.concatenate([moved_real, moved_imag], axis=1).astype(jnp.bfloat16)
    left_side, right_side = inverse_blocks(grid_size)
    halfway = jnp.einsum("ab,fbc->fac", left_side, stacked, preferred_element_type=jnp.float32)
    halfway = halfway.astype(jnp.bfloat16)
    across = jnp.concatenate([halfway[:, :grid_size, :], halfway[:, grid_size:, :]], axis=2)
    regular_image = jnp.einsum(
        "fab,bc->fac", across, right_side, preferred_element_type=jnp.float32
    )
    return regular_image * (1.0 / grid_size)


def place_rows(values, slot_index, tile_count, capacity):
    empty_rows = jnp.zeros((tile_count * capacity, values.shape[1]), values.dtype)
    return empty_rows.at[slot_index].set(values).reshape(tile_count, capacity, values.shape[1])


def per_device(traces, route, mid_x, mid_y, band_low, band_high, offset_bin, azimuth_bin):
    tile_count = lax.axis_size("tile")
    band_count = lax.axis_size("band")
    source_rows = traces.shape[0]
    sample_count = traces.shape[1]
    trace_length = sample_count * band_count
    freq_count = F_DEV * band_count
    capacity = 2 * source_rows // tile_count
    receive = tile_count * capacity
    target = route[:, 0]
    one_hot = (target[:, None] == jnp.arange(tile_count, dtype=jnp.int32)[None, :]).astype(
        jnp.int32
    )
    earlier = jnp.cumsum(one_hot, axis=0) - one_hot
    slot_index = target * capacity + jnp.sum(earlier * one_hot, axis=1)
    midpoints = jnp.stack([mid_x, mid_y], axis=1).astype(jnp.bfloat16)
    arrived = (
        lax.all_to_all(
            place_rows(traces, slot_index, tile_count, capacity),
            "tile",
            split_axis=0,
            concat_axis=0,
            tiled=True,
        ),
        lax.all_to_all(
            place_rows(midpoints, slot_index, tile_count, capacity),
            "tile",
            split_axis=0,
            concat_axis=0,
            tiled=True,
        ),
    )
    arrived_mids = arrived[1].reshape(receive, 2)
    full_time = lax.all_to_all(
        arrived[0].reshape(receive, sample_count), "band", split_axis=0, concat_axis=1, tiled=True
    )
    kernel = time_kernel(trace_length, trace_length, freq_count)
    spectra = jnp.dot(full_time, kernel, preferred_element_type=jnp.float32).astype(jnp.bfloat16)
    result_rows = lax.all_to_all(spectra, "band", split_axis=1, concat_axis=0, tiled=True)
    pos_x = arrived_mids[:, 0].astype(jnp.int32)
    pos_y = arrived_mids[:, 1].astype(jnp.int32)
    real_part, imag_part = accumulate(result_rows, pos_x, pos_y, MIDS, source_rows ** (-0.5))
    first_freq = lax.axis_index("band") * F_DEV
    freq_index = first_freq + jnp.arange(F_DEV, dtype=jnp.int32)
    live_mask = ((freq_index >= band_low[0]) & (freq_index < band_high[0])).astype(jnp.float32)
    omegas = log_omegas(first_freq, F_DEV, trace_length)
    phase_table = amo_phase(omegas, offset_bin[0], azimuth_bin[0], MIDS)
    regular_image = finish(real_part, imag_part, phase_table, live_mask, MIDS)
    return regular_image.reshape(1, F_DEV, MIDS, 2 * MIDS)


def solution(mesh):
    return jax.shard_map(
        per_device,
        mesh=mesh,
        in_specs=(
            P("tile", "band"),
            P("tile", None),
            P("tile"),
            P("tile"),
            P("tile"),
            P("tile"),
            P("tile"),
            P("tile"),
        ),
        out_specs=P("tile", "band", None, None),
        check_vma=False,
    )
```

profile of v0, /device:TPU:32, one launch (start us, length us, event | category | flops | bytes accessed | tf_op | source)
XLA Modules:
  0.0 237.5 jit_solution(18154463155784673148)
XLA Ops:
  0.8 9.1 %reduce-window.6 = s32[32,16,128]{2,1,0:T(8,128)S(1)} reduce-window(s32[32,16,128]{2,1,0:T(8,128)S(1)} %fusion.58, s32[]{:T(128)} %constant.136.clone.1), window={size=1x1x128 pad=0_0x0_0x127_0}, to_apply=%region_0.0 | reduce-window | flops 8323072 | bytes 524292 | tf_op jit(solution)/shard_map/reduce-window
  10.7 7.1 %scatter_custom_fusion = bf16[4096,128]{1,0:T(8,128)(2,1)} fusion(s32[2048]{0:T(1024)S(1)} %bitcast.98, bf16[2048,128]{1,0:T(8,128)(2,1)} %param.10, bf16[]{:T(256)} %constant.138.clone.1), kind=kCustom, calls=%fused_computation.72 | custom fusion | bytes 1049088 | tf_op jit(solution)/shard_map/scatter | solution.py:126
  17.9 11.2 %all-to-all-start = ((bf16[32,128,128]{2,1,0:T(8,128)(2,1)}), bf16[32,128,128]{2,1,0:T(8,128)(2,1)}, u32[]{:S(2)}, u32[]{:S(2)}) async-start(bf16[32,128,128]{2,1,0:T(8,128)(2,1)} %bitcast.7), calls=%async_computation | async-start | bytes 2097152 | tf_op jit(solution)/shard_map/all_to_all | solution.py:146
  29.8 27.9 %all-to-all-done = bf16[32,128,128]{2,1,0:T(8,128)(2,1)} async-done(((bf16[32,128,128]{2,1,0:T(8,128)(2,1)}), bf16[32,128,128]{2,1,0:T(8,128)(2,1)}, u32[]{:S(2)}, u32[]{:S(2)}) %all-to-all-start) | async-done | bytes 1048608 | tf_op jit(solution)/shard_map/all_to_all | solution.py:146
  57.7 4.5 %all-to-all-start.1 = ((bf16[8,512,128]{2,1,0:T(8,128)(2,1)}), bf16[8,512,128]{2,1,0:T(8,128)(2,1)S(1)}, u32[]{:S(2)}, u32[]{:S(2)}) async-start(bf16[8,512,128]{2,1,0:T(8,128)(2,1)} %bitcast.8), calls=%async_computation.1 | async-start | bytes 2097152 | tf_op jit(solution)/shard_map/all_to_all | solution.py:162
  63.5 6.1 %scatter_custom_fusion.1 = bf16[4096,2]{1,0:T(8,128)(2,1)S(1)} fusion(s32[2048]{0:T(1024)S(1)} %bitcast.99, bf16[2048,2]{1,0:T(8,128)(2,1)S(1)} %copy.51, bf16[]{:T(256)} %constant.138.clone.1), kind=kCustom, calls=%fused_computation.70 | custom fusion | bytes 16386 | tf_op jit(solution)/shard_map/scatter | solution.py:126
  73.6 1.8 negate_convert_fusion.1
  75.6 2.6 %all-to-all-done.1 = bf16[8,512,128]{2,1,0:T(8,128)(2,1)S(1)} async-done(((bf16[8,512,128]{2,1,0:T(8,128)(2,1)}), bf16[8,512,128]{2,1,0:T(8,128)(2,1)S(1)}, u32[]{:S(2)}, u32[]{:S(2)}) %all-to-all-start.1) | async-done | bytes 1048608 | tf_op jit(solution)/shard_map/all_to_all | solution.py:162
  78.2 5.2 %all-to-all-start.3 = ((bf16[32,128,2]{1,2,0:T(2,128)(2,1)}), bf16[32,128,2]{1,2,0:T(2,128)(2,1)S(1)}, u32[]{:S(2)}, u32[]{:S(2)}) async-start(bf16[32,128,2]{1,2,0:T(2,128)(2,1)} %copy.52), calls=%async_computation.3 | async-start | bytes 32768 | tf_op jit(solution)/shard_map/all_to_all | solution.py:153
  84.8 7.1 %all-to-all-done.3 = bf16[32,128,2]{1,2,0:T(2,128)(2,1)S(1)} async-done(((bf16[32,128,2]{1,2,0:T(2,128)(2,1)}), bf16[32,128,2]{1,2,0:T(2,128)(2,1)S(1)}, u32[]{:S(2)}, u32[]{:S(2)}) %all-to-all-start.3) | async-done | bytes 16416 | tf_op jit(solution)/shard_map/all_to_all | solution.py:153
  91.9 3.5 %all-to-all-start.2 = ((bf16[512,8,8]{0,2,1:T(8,128)(2,1)}), bf16[512,8,8]{0,2,1:T(8,128)(2,1)S(1)}, u32[]{:S(2)}, u32[]{:S(2)}) async-start(bf16[512,8,8]{0,2,1:T(8,128)(2,1)} %fusion.22), calls=%async_computation.2 | async-start | bytes 131072 | tf_op jit(solution)/shard_map/all_to_all | solution.py:167
  95.5 5.3 %all-to-all-done.2 = bf16[512,8,8]{0,2,1:T(8,128)(2,1)S(1)} async-done(((bf16[512,8,8]{0,2,1:T(8,128)(2,1)}), bf16[512,8,8]{0,2,1:T(8,128)(2,1)S(1)}, u32[]{:S(2)}, u32[]{:S(2)}) %all-to-all-start.2) | async-done | bytes 65568 | tf_op jit(solution)/shard_map/all_to_all | solution.py:167
  100.8 107.6 %while.16 = (s32[]{:T(128)}, f32[2048,512]{1,0:T(8,128)}, bf16[4096,8]{0,1:T(8,128)(2,1)S(1)}, s32[4096]{0:T(1024)S(1)}, s32[4096]{0:T(1024)S(1)}, /*index=5*/s32[]{:T(128)}, s32[]{:T(128)}, s32[]{:T(128)}, s32[]{:T(128)}) while((s32[]{:T(128)}, f32[2048,512]{1,0:T(8,128)}, bf16[4096,8]{0,1:T(8,128)(2,1)S(1)}, s32[4096]{0:T(1024)S(1)}, ...), condition=%wide.region_6.7_spmd.clone, body=%wide.region_5.6_spmd.clone.sunk | while | flops 1089478656 | bytes 24268960 | solution.py:87
  100.9 2.1 fusion.81
  103.5 1.5 subtract_convert_fusion.2
  106.6 2.5 %cosine_convert_fusion.3 = (bf16[512,256]{1,0:T(8,128)(2,1)S(1)}, bf16[512,256]{1,0:T(8,128)(2,1)S(1)}) fusion(s32[512]{0:T(512)S(1)} %dynamic_slice.39), kind=kLoop, calls=%fused_computation.22.clone.1 | loop fusion | flops 2228224 | bytes 526336 | tf_op jit(solution)/shard_map/convert.1
  109.1 3.3 %select_add_fusion.2 = f32[2048,512]{1,0:T(8,128)} fusion(f32[2048,512]{1,0:T(8,128)} %get-tuple-element.248, bf16[512,2048]{1,0:T(8,128)(2,1)S(1)} %bitcast.81, pred[]{:T(512)S(6)} %compare.6, bf16[512,256]{1,0:T(8,128)(2,1)S(1)} %get-tuple-element.236, bf16[512,256]{1,0:T(8,128)(2,1)S(1)} %get-tuple-element.237), kind=kOutput, calls=%fused_computation.2.clone.1 | convolution fusion | flops 1076887552 | bytes 11010049 | tf_op jit(solution)/shard_map/while/body/eval_jaxpr/dot_general | solution.py:82
  112.5 2.1 fusion.81
  115.0 1.5 subtract_convert_fusion.2
  118.2 2.5 %cosine_convert_fusion.3 = (bf16[512,256]{1,0:T(8,128)(2,1)S(1)}, bf16[512,256]{1,0:T(8,128)(2,1)S(1)}) fusion(s32[512]{0:T(512)S(1)} %dynamic_slice.39), kind=kLoop, calls=%fused_computation.22.clone.1 | loop fusion | flops 2228224 | bytes 526336 | tf_op jit(solution)/shard_map/convert.1
  120.7 5.4 %select_add_fusion.2 = f32[2048,512]{1,0:T(8,128)} fusion(f32[2048,512]{1,0:T(8,128)} %get-tuple-element.248, bf16[512,2048]{1,0:T(8,128)(2,1)S(1)} %bitcast.81, pred[]{:T(512)S(6)} %compare.6, bf16[512,256]{1,0:T(8,128)(2,1)S(1)} %get-tuple-element.236, bf16[512,256]{1,0:T(8,128)(2,1)S(1)} %get-tuple-element.237), kind=kOutput, calls=%fused_computation.2.clone.1 | convolution fusion | flops 1076887552 | bytes 11010049 | tf_op jit(solution)/shard_map/while/body/eval_jaxpr/dot_general | solution.py:82
  126.2 2.1 fusion.81
  128.7 1.5 subtract_convert_fusion.2
  131.9 2.5 %cosine_convert_fusion.3 = (bf16[512,256]{1,0:T(8,128)(2,1)S(1)}, bf16[512,256]{1,0:T(8,128)(2,1)S(1)}) fusion(s32[512]{0:T(512)S(1)} %dynamic_slice.39), kind=kLoop, calls=%fused_computation.22.clone.1 | loop fusion | flops 2228224 | bytes 526336 | tf_op jit(solution)/shard_map/convert.1
  134.4 5.4 %select_add_fusion.2 = f32[2048,512]{1,0:T(8,128)} fusion(f32[2048,512]{1,0:T(8,128)} %get-tuple-element.248, bf16[512,2048]{1,0:T(8,128)(2,1)S(1)} %bitcast.81, pred[]{:T(512)S(6)} %compare.6, bf16[512,256]{1,0:T(8,128)(2,1)S(1)} %get-tuple-element.236, bf16[512,256]{1,0:T(8,128)(2,1)S(1)} %get-tuple-element.237), kind=kOutput, calls=%fused_computation.2.clone.1 | convolution fusion | flops 1076887552 | bytes 11010049 | tf_op jit(solution)/shard_map/while/body/eval_jaxpr/dot_general | solution.py:82
  139.9 2.1 fusion.81
  142.4 1.5 subtract_convert_fusion.2
  145.6 2.5 %cosine_convert_fusion.3 = (bf16[512,256]{1,0:T(8,128)(2,1)S(1)}, bf16[512,256]{1,0:T(8,128)(2,1)S(1)}) fusion(s32[512]{0:T(512)S(1)} %dynamic_slice.39), kind=kLoop, calls=%fused_computation.22.clone.1 | loop fusion | flops 2228224 | bytes 526336 | tf_op jit(solution)/shard_map/convert.1
  148.1 5.4 %select_add_fusion.2 = f32[2048,512]{1,0:T(8,128)} fusion(f32[2048,512]{1,0:T(8,128)} %get-tuple-element.248, bf16[512,2048]{1,0:T(8,128)(2,1)S(1)} %bitcast.81, pred[]{:T(512)S(6)} %compare.6, bf16[512,256]{1,0:T(8,128)(2,1)S(1)} %get-tuple-element.236, bf16[512,256]{1,0:T(8,128)(2,1)S(1)} %get-tuple-element.237), kind=kOutput, calls=%fused_computation.2.clone.1 | convolution fusion | flops 1076887552 | bytes 11010049 | tf_op jit(solution)/shard_map/while/body/eval_jaxpr/dot_general | solution.py:82
  153.7 2.1 fusion.81
  159.3 2.5 %cosine_convert_fusion.3 = (bf16[512,256]{1,0:T(8,128)(2,1)S(1)}, bf16[512,256]{1,0:T(8,128)(2,1)S(1)}) fusion(s32[512]{0:T(512)S(1)} %dynamic_slice.39), kind=kLoop, calls=%fused_computation.22.clone.1 | loop fusion | flops 2228224 | bytes 526336 | tf_op jit(solution)/shard_map/convert.1
  161.9 5.4 %select_add_fusion.2 = f32[2048,512]{1,0:T(8,128)} fusion(f32[2048,512]{1,0:T(8,128)} %get-tuple-element.248, bf16[512,2048]{1,0:T(8,128)(2,1)S(1)} %bitcast.81, pred[]{:T(512)S(6)} %compare.6, bf16[512,256]{1,0:T(8,128)(2,1)S(1)} %get-tuple-element.236, bf16[512,256]{1,0:T(8,128)(2,1)S(1)} %get-tuple-element.237), kind=kOutput, calls=%fused_computation.2.clone.1 | convolution fusion | flops 1076887552 | bytes 11010049 | tf_op jit(solution)/shard_map/while/body/eval_jaxpr/dot_general | solution.py:82
  167.4 2.1 fusion.81
  169.9 1.5 subtract_convert_fusion.2
  173.1 2.5 %cosine_convert_fusion.3 = (bf16[512,256]{1,0:T(8,128)(2,1)S(1)}, bf16[512,256]{1,0:T(8,128)(2,1)S(1)}) fusion(s32[512]{0:T(512)S(1)} %dynamic_slice.39), kind=kLoop, calls=%fused_computation.22.clone.1 | loop fusion | flops 2228224 | bytes 526336 | tf_op jit(solution)/shard_map/convert.1
  175.6 5.4 %select_add_fusion.2 = f32[2048,512]{1,0:T(8,128)} fusion(f32[2048,512]{1,0:T(8,128)} %get-tuple-element.248, bf16[512,2048]{1,0:T(8,128)(2,1)S(1)} %bitcast.81, pred[]{:T(512)S(6)} %compare.6, bf16[512,256]{1,0:T(8,128)(2,1)S(1)} %get-tuple-element.236, bf16[512,256]{1,0:T(8,128)(2,1)S(1)} %get-tuple-element.237), kind=kOutput, calls=%fused_computation.2.clone.1 | convolution fusion | flops 1076887552 | bytes 11010049 | tf_op jit(solution)/shard_map/while/body/eval_jaxpr/dot_general | solution.py:82
  181.1 2.1 fusion.81
  186.8 2.5 %cosine_convert_fusion.3 = (bf16[512,256]{1,0:T(8,128)(2,1)S(1)}, bf16[512,256]{1,0:T(8,128)(2,1)S(1)}) fusion(s32[512]{0:T(512)S(1)} %dynamic_slice.39), kind=kLoop, calls=%fused_computation.22.clone.1 | loop fusion | flops 2228224 | bytes 526336 | tf_op jit(solution)/shard_map/convert.1
  189.3 5.4 %select_add_fusion.2 = f32[2048,512]{1,0:T(8,128)} fusion(f32[2048,512]{1,0:T(8,128)} %get-tuple-element.248, bf16[512,2048]{1,0:T(8,128)(2,1)S(1)} %bitcast.81, pred[]{:T(512)S(6)} %compare.6, bf16[512,256]{1,0:T(8,128)(2,1)S(1)} %get-tuple-element.236, bf16[512,256]{1,0:T(8,128)(2,1)S(1)} %get-tuple-element.237), kind=kOutput, calls=%fused_computation.2.clone.1 | convolution fusion | flops 1076887552 | bytes 11010049 | tf_op jit(solution)/shard_map/while/body/eval_jaxpr/dot_general | solution.py:82
  194.8 2.1 fusion.81
  200.5 2.5 %cosine_convert_fusion.3 = (bf16[512,256]{1,0:T(8,128)(2,1)S(1)}, bf16[512,256]{1,0:T(8,128)(2,1)S(1)}) fusion(s32[512]{0:T(512)S(1)} %dynamic_slice.39), kind=kLoop, calls=%fused_computation.22.clone.1 | loop fusion | flops 2228224 | bytes 526336 | tf_op jit(solution)/shard_map/convert.1
  203.0 5.4 %select_add_fusion.2 = f32[2048,512]{1,0:T(8,128)} fusion(f32[2048,512]{1,0:T(8,128)} %get-tuple-element.248, bf16[512,2048]{1,0:T(8,128)(2,1)S(1)} %bitcast.81, pred[]{:T(512)S(6)} %compare.6, bf16[512,256]{1,0:T(8,128)(2,1)S(1)} %get-tuple-element.236, bf16[512,256]{1,0:T(8,128)(2,1)S(1)} %get-tuple-element.237), kind=kOutput, calls=%fused_computation.2.clone.1 | convolution fusion | flops 1076887552 | bytes 11010049 | tf_op jit(solution)/shard_map/while/body/eval_jaxpr/dot_general | solution.py:82
  208.5 5.9 %reshape.327 = f32[4,2,256,2,256]{4,3,2,1,0:T(2,128)} reshape(f32[2048,512]{1,0:T(8,128)} %get-tuple-element.138) | data formatting | bytes 8388608 | tf_op jit(solution)/shard_map/reshape | solution.py:88
  214.4 7.5 %fusion.71 = (f32[4,1,256,1,256]{4,3,2,1,0:T(1,128)S(1)}, f32[4,1,256,1,256]{4,3,2,1,0:T(1,128)}, f32[4,1,256,1,256]{4,3,2,1,0:T(1,128)S(1)}, f32[4,1,256,1,256]{4,3,2,1,0:T(1,128)}) fusion(f32[4,2,256,2,256]{4,3,2,1,0:T(2,128)} %reshape.327), kind=kLoop, calls=%fused_computation.120 | loop fusion | bytes 8388608 | tf_op jit(solution)/shard_map/slice | solution.py:89
  223.2 2.3 copy.64
  225.6 3.6 %copy.65 = f32[4,1,256,1,256]{2,4,0,3,1:T(8,128)} copy(f32[4,1,256,1,256]{4,3,2,1,0:T(1,128)} %get-tuple-element.180) | data formatting | bytes 2097152
  229.2 5.5 %fusion.25 = (bf16[4,256,256]{1,2,0:T(8,128)(2,1)S(1)}, bf16[4,256,256]{1,2,0:T(8,128)(2,1)S(1)}) fusion(f32[4]{0:T(128)S(1)} %and_convert_fusion, f32[256,256]{0,1:T(8,128)S(1)} %log-plus-one_subtract_fusion, f32[4]{0:T(128)S(1)} %convert_multiply_fusion, f32[4,1,256,1,256]{2,4,0,3,1:T(8,128)S(1)} %copy.64, f32[4,1,256,1,256]{2,4,0,3,1:T(8,128)} %copy.65, ...), kind=kLoop, calls=%fused_computation.48 | loop fusion | flops 3407872 | bytes 5505056 | tf_op jit(solution)/shard_map/convert.19
  235.5 2.1 multiply_bitcast_fusion
  (119 shorter events, 29.3 us)
Async XLA Ops:
  0.0 10.6 %copy-start.2 = (s32[2048,1]{0,1:T(1,128)S(1)}, s32[2048,1]{0,1:T(1,128)}, u32[]{:S(2)}) copy-start(s32[2048,1]{0,1:T(1,128)} %param.11) | copy-start | bytes 24580
  10.0 19.1 %copy-start.3 = (s32[2048]{0:T(1024)S(1)}, s32[2048]{0:T(1024)}, u32[]{:S(2)}) copy-start(s32[2048]{0:T(1024)} %param.12) | copy-start | bytes 24580
  10.3 18.9 %copy-start.4 = (s32[2048]{0:T(1024)S(1)}, s32[2048]{0:T(1024)}, u32[]{:S(2)}) copy-start(s32[2048]{0:T(1024)} %param.13) | copy-start | bytes 24580
  17.9 39.8 %all-to-all-start = ((bf16[32,128,128]{2,1,0:T(8,128)(2,1)}), bf16[32,128,128]{2,1,0:T(8,128)(2,1)}, u32[]{:S(2)}, u32[]{:S(2)}) async-start(bf16[32,128,128]{2,1,0:T(8,128)(2,1)} %bitcast.7), calls=%async_computation | async-start | bytes 2097152 | tf_op jit(solution)/shard_map/all_to_all | solution.py:146
  57.7 20.4 %all-to-all-start.1 = ((bf16[8,512,128]{2,1,0:T(8,128)(2,1)}), bf16[8,512,128]{2,1,0:T(8,128)(2,1)S(1)}, u32[]{:S(2)}, u32[]{:S(2)}) async-start(bf16[8,512,128]{2,1,0:T(8,128)(2,1)} %bitcast.8), calls=%async_computation.1 | async-start | bytes 2097152 | tf_op jit(solution)/shard_map/all_to_all | solution.py:162
  78.2 13.8 %all-to-all-start.3 = ((bf16[32,128,2]{1,2,0:T(2,128)(2,1)}), bf16[32,128,2]{1,2,0:T(2,128)(2,1)S(1)}, u32[]{:S(2)}, u32[]{:S(2)}) async-start(bf16[32,128,2]{1,2,0:T(2,128)(2,1)} %copy.52), calls=%async_computation.3 | async-start | bytes 32768 | tf_op jit(solution)/shard_map/all_to_all | solution.py:153
  91.9 8.9 %all-to-all-start.2 = ((bf16[512,8,8]{0,2,1:T(8,128)(2,1)}), bf16[512,8,8]{0,2,1:T(8,128)(2,1)S(1)}, u32[]{:S(2)}, u32[]{:S(2)}) async-start(bf16[512,8,8]{0,2,1:T(8,128)(2,1)} %fusion.22), calls=%async_computation.2 | async-start | bytes 131072 | tf_op jit(solution)/shard_map/all_to_all | solution.py:167
  229.2 5.5 %copy-start = (bf16[256,256]{1,0:T(8,128)(2,1)S(1)}, bf16[256,256]{1,0:T(8,128)(2,1)}, u32[]{:S(2)}) copy-start(bf16[256,256]{1,0:T(8,128)(2,1)} %get-tuple-element.189) | copy-start | bytes 393220
  229.2 5.5 %copy-start.1 = (bf16[256,256]{1,0:T(8,128)(2,1)S(1)}, bf16[256,256]{1,0:T(8,128)(2,1)}, u32[]{:S(2)}) copy-start(bf16[256,256]{1,0:T(8,128)(2,1)} %get-tuple-element.190) | copy-start | bytes 393220
where the time goes:
time: 241 us; the launch traced here: 238 us
  other arithmetic  76.4 us (32%)
  matrix products  45.1 us (19%)
  local copies, waits for them, and re-layouts  45 us (19%)
  waiting for transfers between devices  42.9 us (18%)
  starting transfers between devices  24.4 us (10%)
  between operations  3.07 us (1%)
    another operation x25, other arithmetic  50.6 us
    dot_general x8, matrix products, add_rows(): lax.dot_general(left_rows, right_rows, (((0,), (0,)), ((), ())), preferre...  41.3 us
    all_to_all x1, waiting for transfers between devices, per_device(): lax.all_to_all(place_rows(traces, slot_index, tile_count, capacity), 'til...  27.9 us
    cos x8, other arithmetic, forward_rows(): return (jnp.cos(angles), -jnp.sin(angles))  17.1 us
    scatter x2, local copies, waits for them, and re-layouts, place_rows(): empty_rows.at[slot_index].set(values)  13.2 us
    all_to_all x1, starting transfers between devices, per_device(): lax.all_to_all(place_rows(traces, slot_index, tile_count, capacity), 'til...  11.2 us
    slice x1, local copies, waits for them, and re-layouts, accumulate(): real_part = running[:, 0, :, 0, :] - running[:, 1, :, 1, :]  7.5 us
    unnamed x14, local copies, waits for them, and re-layouts  7.27 us
  transfers between devices with their start and end apart: 4, of which 4 were waited for; matrix products, arithmetic and copies ran while one was open for 5% of the time, Pallas kernels for 0%

commit v1 on v0

v1 whole, which is shorter than its diff:
```python
import math

import jax
import jax.numpy as jnp
import numpy as np
from jax import lax
from jax.experimental import pallas as pl
from jax.experimental.pallas import tpu as pltpu
from jax.sharding import PartitionSpec as P

MIDS = 256
HALF = 128
AZIMUTHS = 12
F_DEV = 4
COLS = 2 * F_DEV
BANDS = 8
TILES = 32
ROWS = 2048
SAMPLES = 128
NT = 1024
CAP = 128
ANCHOR = 64.0
LOG_SPAN = math.log((NT + ANCHOR) / ANCHOR)
CHUNK = 4
NT_DIMS = (((1,), (1,)), ((), ()))
VMEM_BYTES = 56 * 1024 * 1024


def time_kernel_blocks():
    stretch = np.log((np.arange(NT) + ANCHOR) / ANCHOR)
    omegas = (np.arange(F_DEV * BANDS) + 1) * (2.0 * math.pi / LOG_SPAN)
    angles = omegas[:, None] * stretch[None, :]
    stacked = np.stack([np.cos(angles), -np.sin(angles)], axis=1) * NT**-0.5
    stacked = stacked.reshape(COLS * BANDS, BANDS, SAMPLES).transpose(1, 0, 2)
    return stacked.astype(np.float32).astype(jnp.bfloat16)


def folded_table():
    turns = (np.arange(MIDS)[:, None] * np.arange(HALF)[None, :]) % MIDS
    angles = turns * (2.0 * math.pi / MIDS)
    sines = np.sin(angles)
    sines[:, 0] = (-1.0) ** np.arange(MIDS)
    table = np.concatenate([np.cos(angles), sines], axis=1)
    return table.astype(np.float32).astype(jnp.bfloat16)


def sincos_turns(turns):
    quarters = (turns - jnp.round(turns)) * 4.0
    quadrant = jnp.round(quarters)
    angle = (quarters - quadrant) * (math.pi / 2)
    square = angle * angle
    sine = angle * (1.0 + square * (-1.0 / 6 + square * (1.0 / 120 + square * (-1.0 / 5040))))
    cosine = 1.0 + square * (
        -0.5 + square * (1.0 / 24 + square * (-1.0 / 720 + square * (1.0 / 40320)))
    )
    index = quadrant.astype(jnp.int32)
    odd = (index & 1) == 1
    low, high = jnp.where(odd, sine, cosine), jnp.where(odd, cosine, sine)
    cos_out = jnp.where(((index + 1) & 2) == 2, -low, low)
    sin_out = jnp.where((index & 2) == 2, -high, high)
    return cos_out, sin_out


def partial_kernel(kern_hbm, traces_hbm, out_ref, kern, rows, sems):
    band = lax.axis_index("band")
    get_kern = pltpu.make_async_copy(kern_hbm.at[band], kern, sems.at[0])
    get_rows = pltpu.make_async_copy(traces_hbm, rows, sems.at[1])
    get_kern.start()
    get_rows.start()
    get_kern.wait()
    get_rows.wait()
    part = lax.dot_general(kern[...], rows[...], NT_DIMS, preferred_element_type=jnp.float32)
    half = ROWS // 2
    for b in range(BANDS):
        block = part[b * COLS : (b + 1) * COLS]
        out_ref[b] = jnp.concatenate([block[:, :half], block[:, half:]], axis=0).astype(
            jnp.bfloat16
        )


def signed_folded(shape, dim):
    index = lax.broadcasted_iota(jnp.int32, shape, dim)
    signed = jnp.where(index < HALF, index, jnp.where(index == HALF, -HALF, HALF - index))
    return signed.astype(jnp.float32) * (2.0 * math.pi / MIDS)


def tables_kernel(
    route_ref, low_ref, high_ref, offset_ref, azimuth_ref, trig_ref, slot_ref, phase_ref
):
    block = MIDS
    row_i = lax.broadcasted_iota(jnp.int32, (block, block), 0)
    col_i = lax.broadcasted_iota(jnp.int32, (block, block), 1)
    upper = jnp.where(row_i < col_i, 1.0, 0.0).astype(jnp.bfloat16)
    tile_i = lax.broadcasted_iota(jnp.int32, (TILES, block), 0)
    slot_i = lax.broadcasted_iota(jnp.int32, (CAP, block), 0)
    carry = jnp.zeros((TILES, 1), jnp.float32)
    for step in range(ROWS // block):
        cut = slice(step * block, (step + 1) * block)
        member = jnp.where(tile_i == route_ref[:, cut], 1.0, 0.0)
        earlier = jnp.dot(
            member.astype(jnp.bfloat16), upper, preferred_element_type=jnp.float32
        )
        rank = jnp.sum(member * (earlier + carry), axis=0, keepdims=True).astype(jnp.int32)
        slot_ref[:, cut] = jnp.where(slot_i == rank, 1.0, 0.0).astype(jnp.bfloat16)
        carry = carry + jnp.sum(member, axis=1, keepdims=True)
    band = lax.axis_index("band")
    first = band * F_DEV
    h = (offset_ref[0].astype(jnp.float32) + 1.0) * 0.5
    kx = signed_folded((MIDS, MIDS), 0)
    ky = signed_folded((MIDS, MIDS), 1)
    inline = kx * (h * trig_ref[0]) + ky * (h * trig_ref[1])
    along = kx * h
    change = jnp.log1p(along * along) - jnp.log1p(inline * inline)
    unit = change * (0.5 / LOG_SPAN)
    turn_c, turn_s = sincos_turns(unit)
    cos_f, sin_f = sincos_turns(unit * (first + 1).astype(jnp.float32))
    scale = ROWS**-0.5 / MIDS
    for f in range(F_DEV):
        live = (first + f >= low_ref[0]) & (first + f < high_ref[0])
        weight = jnp.where(live, scale, 0.0)
        phase_ref[0, f] = cos_f * weight
        phase_ref[1, f] = sin_f * weight
        if f + 1 < F_DEV:
            cos_f, sin_f = cos_f * turn_c - sin_f * turn_s, cos_f * turn_s + sin_f * turn_c


def place_kernel(part_ref, slot_ref, route_ref, x_ref, y_ref, out_ref, masked):
    total = part_ref[0].astype(jnp.float32)
    for b in range(1, BANDS):
        total = total + part_ref[b].astype(jnp.float32)
    total = total.astype(jnp.bfloat16).astype(jnp.float32)
    spectra = jnp.concatenate([total[:COLS], total[COLS:]], axis=1)
    row = lax.broadcasted_iota(jnp.int32, (8, ROWS), 0)
    mids = jnp.where(
        row == 0, x_ref[...].astype(jnp.float32), jnp.where(row == 1, y_ref[...].astype(jnp.float32), 0.0)
    )
    values = jnp.concatenate([spectra, mids], axis=0)
    tile = jnp.broadcast_to(route_ref[...], (16, ROWS))
    for g in range(TILES):
        masked[g * 16 : (g + 1) * 16, :] = jnp.where(tile == g, values, 0.0).astype(jnp.bfloat16)
    placed = lax.dot_general(
        masked[...], slot_ref[...], NT_DIMS, preferred_element_type=jnp.float32
    )
    out_ref[...] = placed.astype(jnp.bfloat16).reshape(TILES, 16, CAP)


def tile_kernel(
    got_ref,
    table_hbm,
    tablet_hbm,
    phase_hbm,
    out_hbm,
    xa,
    xb,
    ya,
    yb,
    acc,
    table,
    tablet,
    phase,
    image,
    sems,
):
    copies = [
        pltpu.make_async_copy(table_hbm, table, sems.at[0]),
        pltpu.make_async_copy(tablet_hbm, tablet, sems.at[1]),
        pltpu.make_async_copy(phase_hbm, phase, sems.at[2]),
    ]
    for copy in copies:
        copy.start()
    iota = lax.broadcasted_iota(jnp.int32, (16, CAP), 0).astype(jnp.float32)
    one = jnp.ones((16, CAP), jnp.bfloat16)
    zero = jnp.zeros((16, CAP), jnp.bfloat16)

    def build(x_buf, y_buf, step):
        for i in range(CHUNK):
            part = got_ref[step * CHUNK + i].astype(jnp.float32)
            rows = [
                jnp.broadcast_to(part[c : c + 1], (16, CAP)).astype(jnp.bfloat16)
                for c in range(COLS + 2)
            ]
            cut = slice(i * CAP, (i + 1) * CAP)
            for r in range(MIDS // 16):
                here = (iota + (16.0 * r)).astype(jnp.bfloat16)
                in_x = here == rows[COLS]
                for c in range(COLS):
                    at = c * MIDS + r * 16
                    x_buf[at : at + 16, cut] = jnp.where(in_x, rows[c], zero)
                y_buf[r * 16 : (r + 1) * 16, cut] = jnp.where(here == rows[COLS + 1], one, zero)

    def add(x_buf, y_buf):
        acc[...] += lax.dot_general(
            x_buf[...], y_buf[...], NT_DIMS, preferred_element_type=jnp.float32
        )

    acc[...] = jnp.zeros_like(acc)
    steps = TILES // CHUNK
    build(xa, ya, 0)

    def pair(p, _):
        build(xb, yb, 2 * p + 1)
        add(xa, ya)
        build(xa, ya, jnp.minimum(2 * p + 2, steps - 1))
        add(xb, yb)
        return 0

    lax.fori_loop(0, steps // 2, pair, 0)
    for copy in copies:
        copy.wait()

    lane0 = lax.broadcasted_iota(jnp.int32, (MIDS, HALF), 1) == 0
    row0 = lax.broadcasted_iota(jnp.int32, (HALF, MIDS), 0) == 0
    bf = lambda v: v.astype(jnp.bfloat16)
    dot = lambda a, b: jnp.dot(a, b, preferred_element_type=jnp.float32)
    puts = []
    for f in range(F_DEV):
        u = dot(bf(acc[f * 512 : (f + 1) * 512]), table[...])
        cr, sr, ci, si = u[:MIDS, :HALF], u[:MIDS, HALF:], u[MIDS:, :HALF], u[MIDS:, HALF:]
        sr0, si0 = jnp.where(lane0, 0.0, sr), jnp.where(lane0, 0.0, si)
        h_r = [cr + si0, jnp.where(lane0, sr, cr - si)]
        h_i = [ci - sr0, jnp.where(lane0, si, ci + sr)]
        h = bf(jnp.concatenate(h_r + h_i, axis=1))
        v = dot(tablet[...], h)
        cr, sr, ci, si = v[:HALF, :MIDS], v[HALF:, :MIDS], v[:HALF, MIDS:], v[HALF:, MIDS:]
        sr0, si0 = jnp.where(row0, 0.0, sr), jnp.where(row0, 0.0, si)
        wpr, wpi = cr + si0, ci - sr0
        wmr, wmi = jnp.where(row0, sr, cr - si), jnp.where(row0, si, ci + sr)
        pc, ps = phase[0, f, :HALF], phase[1, f, :HALF]
        mc, ms = phase[0, f, HALF:], phase[1, f, HALF:]
        mpr, mpi = wpr * pc - wpi * ps, wpr * ps + wpi * pc
        mmr, mmi = wmr * mc - wmi * ms, wmr * ms + wmi * mc
        a_r = mpr + jnp.where(row0, 0.0, mmr)
        a_i = mpi + jnp.where(row0, 0.0, mmi)
        d_r = jnp.where(row0, mmr, mmi - mpi)
        d_i = jnp.where(row0, mmi, mpr - mmr)
        folded = jnp.concatenate(
            [jnp.concatenate([a_r, a_i], axis=1), jnp.concatenate([d_r, d_i], axis=1)], axis=0
        )
        q = dot(table[...], bf(folded))
        qpr, qmr, qpi, qmi = q[:, :HALF], q[:, HALF:MIDS], q[:, MIDS : MIDS + HALF], q[:, MIDS + HALF :]
        a_r = qpr + jnp.where(lane0, 0.0, qmr)
        a_i = qpi + jnp.where(lane0, 0.0, qmi)
        d_r = jnp.where(lane0, qmr, qmi - qpi)
        d_i = jnp.where(lane0, qmi, qpr - qmr)
        folded = jnp.concatenate(
            [jnp.concatenate([a_r, d_r], axis=1), jnp.concatenate([a_i, d_i], axis=1)], axis=0
        )
        w = dot(bf(folded), tablet[...])
        image[f, :, :MIDS] = w[:MIDS]
        image[f, :, MIDS:] = w[MIDS:]
        put = pltpu.make_async_copy(image.at[f], out_hbm.at[f], sems.at[3 + f])
        put.start()
        puts.append(put)
    for put in puts:
        put.wait()


VM = pl.BlockSpec(memory_space=pltpu.VMEM)
SM = pl.BlockSpec(memory_space=pltpu.SMEM)
ANY = pl.BlockSpec(memory_space=pl.ANY)
PARAMS = pltpu.CompilerParams(vmem_limit_bytes=VMEM_BYTES)


def cost(flops, moved):
    return pl.CostEstimate(flops=flops, bytes_accessed=moved, transcendentals=0)


def partial_spectra(kern, traces):
    return pl.pallas_call(
        partial_kernel,
        out_shape=jax.ShapeDtypeStruct((BANDS, 16, ROWS // 2), jnp.bfloat16),
        in_specs=[ANY, ANY],
        out_specs=VM,
        scratch_shapes=[
            pltpu.VMEM((COLS * BANDS, SAMPLES), jnp.bfloat16),
            pltpu.VMEM((ROWS, SAMPLES), jnp.bfloat16),
            pltpu.SemaphoreType.DMA((2,)),
        ],
        compiler_params=PARAMS,
        cost_estimate=cost(2 * 64 * SAMPLES * ROWS, 800_000),
        name="partial_spectra",
    )(kern, traces)


def slot_and_phase(route, low, high, offset, azimuth, trig):
    return pl.pallas_call(
        tables_kernel,
        out_shape=(
            jax.ShapeDtypeStruct((CAP, ROWS), jnp.bfloat16),
            jax.ShapeDtypeStruct((2, F_DEV, MIDS, MIDS), jnp.float32),
        ),
        in_specs=[VM, SM, SM, SM, SM, SM],
        out_specs=(VM, VM),
        compiler_params=PARAMS,
        cost_estimate=cost(2_000_000_000, 3_000_000),
        name="slot_and_phase",
    )(route, low, high, offset, azimuth, trig)


def place(part, slots, route, mid_x, mid_y):
    return pl.pallas_call(
        place_kernel,
        out_shape=jax.ShapeDtypeStruct((TILES, 16, CAP), jnp.bfloat16),
        in_specs=[VM] * 5,
        out_specs=VM,
        scratch_shapes=[pltpu.VMEM((TILES * 16, ROWS), jnp.bfloat16)],
        compiler_params=PARAMS,
        cost_estimate=cost(2 * 512 * ROWS * CAP, 1_000_000),
        name="place",
    )(part, slots, route, mid_x, mid_y)


def tile_image(got, table, tablet, phase):
    return pl.pallas_call(
        tile_kernel,
        out_shape=jax.ShapeDtypeStruct((F_DEV, MIDS, 2 * MIDS), jnp.float32),
        in_specs=[VM, ANY, ANY, ANY],
        out_specs=ANY,
        scratch_shapes=[
            pltpu.VMEM((COLS * MIDS, CHUNK * CAP), jnp.bfloat16),
            pltpu.VMEM((COLS * MIDS, CHUNK * CAP), jnp.bfloat16),
            pltpu.VMEM((MIDS, CHUNK * CAP), jnp.bfloat16),
            pltpu.VMEM((MIDS, CHUNK * CAP), jnp.bfloat16),
            pltpu.VMEM((COLS * MIDS, MIDS), jnp.float32),
            pltpu.VMEM((MIDS, MIDS), jnp.bfloat16),
            pltpu.VMEM((MIDS, MIDS), jnp.bfloat16),
            pltpu.VMEM((2, F_DEV, MIDS, MIDS), jnp.float32),
            pltpu.VMEM((F_DEV, MIDS, 2 * MIDS), jnp.float32),
            pltpu.SemaphoreType.DMA((3 + F_DEV,)),
        ],
        compiler_params=PARAMS,
        cost_estimate=cost(6_000_000_000, 5_000_000),
        name="tile_image",
    )(got, table, tablet, phase)


def per_device(traces, route, mid_x, mid_y, band_low, band_high, offset_bin, azimuth_bin):
    table = folded_table()
    route = route.reshape(1, ROWS)
    mid_x = mid_x.reshape(1, ROWS)
    mid_y = mid_y.reshape(1, ROWS)
    theta = azimuth_bin.astype(jnp.float32) * (math.pi / AZIMUTHS)
    trig = jnp.concatenate([jnp.cos(theta), jnp.sin(theta)])
    part = partial_spectra(jnp.asarray(time_kernel_blocks()), traces)
    part = lax.all_to_all(part, "band", split_axis=0, concat_axis=0, tiled=True)
    slots, phase = slot_and_phase(route, band_low, band_high, offset_bin, azimuth_bin, trig)
    sent = place(part, slots, route, mid_x, mid_y)
    got = lax.all_to_all(sent, "tile", split_axis=0, concat_axis=0, tiled=True)
    image = tile_image(got, jnp.asarray(table), jnp.asarray(np.ascontiguousarray(table.T)), phase)
    return image[None]


def solution(mesh):
    return jax.shard_map(
        per_device,
        mesh=mesh,
        in_specs=(
            P("tile", "band"),
            P("tile", None),
            P("tile"),
            P("tile"),
            P("tile"),
            P("tile"),
            P("tile"),
            P("tile"),
        ),
        out_specs=P("tile", "band", None, None),
        check_vma=False,
    )
```

time: 241 us -> 50.5 us (0.21)
  the two profiles are of different devices: /device:TPU:32 before, /device:TPU:8 now
where the time goes in v1:
time: 50.5 us; the launch traced here: 50.1 us
  blocking collectives  21.5 us (43%)
  Pallas kernels  19 us (38%)
  starting transfers between devices  5.51 us (11%)
  between operations  2.76 us (5%)
  local copies, waits for them, and re-layouts  0.72 us (1%)
  other arithmetic  0.66 us (1%)
    all_to_all x1, blocking collectives, per_device(): got = lax.all_to_all(sent, 'tile', split_axis=0, concat_axis=0, tiled=True)  21.5 us
    pallas_call x1, Pallas kernels, tile_image(): pl.pallas_call(tile_kernel, out_shape=jax.ShapeDtypeStruct((F_DEV, MIDS,...  10.8 us
    all_to_all x1, starting transfers between devices, per_device(): part = lax.all_to_all(part, 'band', split_axis=0, concat_axis=0, tiled=True)  5.51 us
    pallas_call x1, Pallas kernels, slot_and_phase(): pl.pallas_call(tables_kernel, out_shape=(jax.ShapeDtypeStruct((CAP, ROWS)...  3.64 us
    pallas_call x1, Pallas kernels, place(): pl.pallas_call(place_kernel, out_shape=jax.ShapeDtypeStruct((TILES, 16, C...  2.48 us
    pallas_call x1, Pallas kernels, partial_spectra(): pl.pallas_call(partial_kernel, out_shape=jax.ShapeDtypeStruct((BANDS, 16,...  2.09 us
  transfers between devices with their start and end apart: 1, of which 0 were waited for; matrix products, arithmetic and copies ran while one was open for 1% of the time, Pallas kernels for 7%

profile of v1, /device:TPU:8, one launch (start us, length us, event | category | flops | bytes accessed | tf_op | source)
XLA Modules:
  0.0 50.1 jit_solution(16744708152421414603)
XLA Ops:
  0.0 2.1 %partial_spectra.1 = bf16[8,16,1024]{2,1,0:T(8,128)(2,1)} custom-call(bf16[8,64,128]{2,1,0:T(8,128)(2,1)} %constant.8.clone.kern_hbm, bf16[2048,128]{1,0:T(8,128)(2,1)} %traces_hbm.1), custom_call_target="tpu_custom_call" | custom-call | flops 33554432 | bytes 800000 | tf_op jit(solution)/shard_map/partial_spectra/pallas_call | solution.py:269
  2.1 5.5 %all-to-all-start = ((bf16[8,16,1024]{2,1,0:T(8,128)(2,1)}), bf16[8,16,1024]{2,1,0:T(8,128)(2,1)S(1)}, u32[]{:S(2)}, u32[]{:S(2)}) async-start(bf16[8,16,1024]{2,1,0:T(8,128)(2,1)} %partial_spectra.1), calls=%async_computation | async-start | bytes 524288 | tf_op jit(solution)/shard_map/all_to_all | solution.py:345
  8.4 0.7 %pad_maximum_fusion.trig_ref = f32[2]{0:T(128)} fusion(f32[1]{0:T(128)S(6)} %sin.3, f32[1]{0:T(128)S(6)} %cos.3), kind=kLoop, calls=%fused_computation | loop fusion | flops 2 | bytes 16 | tf_op jit(solution)/shard_map/concatenate | solution.py:343
  11.0 3.6 %slot_and_phase.1 = (bf16[128,2048]{1,0:T(8,128)(2,1)}, f32[2,4,256,256]{3,2,1,0:T(8,128)}) custom-call(s32[1,2048]{1,0:T(1,128)} %bitcast.4, s32[1]{0:T(128)S(6)} %copy.12.low_ref, s32[1]{0:T(128)S(6)} %copy.13.high_ref, s32[1]{0:T(128)S(6)} %copy.14.offset_ref, s32[1]{0:T(128)S(6)} %copy.15.azimuth_ref, f32[2]{0:T(128)} %pad_maximum_fusion.trig_ref), custom_call_target="tpu_custom_call" | custom-call | flops 2000000000 | bytes 3000000 | tf_op jit(solution)/shard_map/slot_and_phase/pallas_call | solution.py:286
  14.7 0.0 all-to-all-done.part_ref
  14.7 0.0 copy-start
  14.7 0.7 %copy-done = bf16[8,16,1024]{2,1,0:T(8,128)(2,1)} copy-done((bf16[8,16,1024]{2,1,0:T(8,128)(2,1)}, bf16[8,16,1024]{2,1,0:T(8,128)(2,1)S(1)}, u32[]{:S(2)}) %copy-start) | copy-done | bytes 262168
  15.4 2.5 %place.1 = bf16[32,16,128]{2,1,0:T(8,128)(2,1)} custom-call(bf16[8,16,1024]{2,1,0:T(8,128)(2,1)} %copy-done, bf16[128,2048]{1,0:T(8,128)(2,1)} %get-tuple-element.7.slot_ref, s32[1,2048]{1,0:T(1,128)} %bitcast.5, s32[1,2048]{1,0:T(1,128)} %bitcast.6, s32[1,2048]{1,0:T(1,128)} %bitcast.7), custom_call_target="tpu_custom_call" | custom-call | flops 268435456 | bytes 1000000 | tf_op jit(solution)/shard_map/place/pallas_call | solution.py:301
  17.9 21.5 %all_to_all.10.got_ref = bf16[32,16,128]{2,1,0:T(8,128)(2,1)} all-to-all(bf16[32,16,128]{2,1,0:T(8,128)(2,1)} %place.1), channel_id=1, replica_groups=mesh['tile'=32,'band'=8] {'tile'}, dimensions={0} | all-to-all | bytes 262144 | tf_op jit(solution)/shard_map/all_to_all | solution.py:348
  39.3 10.8 %tile_image.1 = f32[4,256,512]{2,1,0:T(8,128)} custom-call(bf16[32,16,128]{2,1,0:T(8,128)(2,1)} %all_to_all.10.got_ref, bf16[256,256]{1,0:T(8,128)(2,1)} %constant.9.clone.table_hbm, bf16[256,256]{1,0:T(8,128)(2,1)} %constant.10.clone.tablet_hbm, f32[2,4,256,256]{3,2,1,0:T(8,128)} %get-tuple-element.8.phase_hbm), custom_call_target="tpu_custom_call" | custom-call | flops 6000000000 | bytes 5000000 | tf_op jit(solution)/shard_map/tile_image/pallas_call | solution.py:314
Async XLA Ops:
  2.1 12.6 %all-to-all-start = ((bf16[8,16,1024]{2,1,0:T(8,128)(2,1)}), bf16[8,16,1024]{2,1,0:T(8,128)(2,1)S(1)}, u32[]{:S(2)}, u32[]{:S(2)}) async-start(bf16[8,16,1024]{2,1,0:T(8,128)(2,1)} %partial_spectra.1), calls=%async_computation | async-start | bytes 524288 | tf_op jit(solution)/shard_map/all_to_all | solution.py:345
  14.7 0.7 %copy-start = (bf16[8,16,1024]{2,1,0:T(8,128)(2,1)}, bf16[8,16,1024]{2,1,0:T(8,128)(2,1)S(1)}, u32[]{:S(2)}) copy-start(bf16[8,16,1024]{2,1,0:T(8,128)(2,1)S(1)} %all-to-all-done.part_ref) | copy-start | bytes 786436

commit v2 on v1

v2 whole, which is shorter than its diff:
```python
import math

import jax
import jax.numpy as jnp
import numpy as np
from jax import lax
from jax.experimental import pallas as pl
from jax.experimental.pallas import tpu as pltpu
from jax.sharding import PartitionSpec as P

MIDS = 256
HALF = 128
AZIMUTHS = 12
F_DEV = 4
COLS = 2 * F_DEV
BANDS = 8
TILES = 32
ROWS = 2048
SAMPLES = 128
NT = 1024
CAP = 128
ANCHOR = 64.0
LOG_SPAN = math.log((NT + ANCHOR) / ANCHOR)
CLASSES = 4
WIDE = MIDS // CLASSES
PARTS = 8
SPAN = CAP // PARTS
DEPTH = TILES * SPAN
PIECES = 1
PIECE = ROWS // PIECES
NT_DIMS = (((1,), (1,)), ((), ()))


def time_kernel_blocks():
    stretch = np.log((np.arange(NT) + ANCHOR) / ANCHOR)
    omegas = (np.arange(F_DEV * BANDS) + 1) * (2.0 * math.pi / LOG_SPAN)
    angles = omegas[:, None] * stretch[None, :]
    stacked = np.stack([np.cos(angles), -np.sin(angles)], axis=1) * NT**-0.5
    stacked = stacked.reshape(COLS * BANDS, BANDS, SAMPLES).transpose(1, 0, 2)
    return stacked.astype(np.float32).astype(jnp.bfloat16)


def folded_table():
    turns = (np.arange(MIDS)[:, None] * np.arange(HALF)[None, :]) % MIDS
    angles = turns * (2.0 * math.pi / MIDS)
    sines = np.sin(angles)
    sines[:, 0] = (-1.0) ** np.arange(MIDS)
    table = np.concatenate([np.cos(angles), sines], axis=1)
    return table.astype(np.float32).astype(jnp.bfloat16)


def sincos_turns(turns):
    quarters = (turns - jnp.round(turns)) * 4.0
    quadrant = jnp.round(quarters)
    angle = (quarters - quadrant) * (math.pi / 2)
    square = angle * angle
    sine = angle * (1.0 + square * (-1.0 / 6 + square * (1.0 / 120 + square * (-1.0 / 5040))))
    cosine = 1.0 + square * (
        -0.5 + square * (1.0 / 24 + square * (-1.0 / 720 + square * (1.0 / 40320)))
    )
    index = quadrant.astype(jnp.int32)
    odd = (index & 1) == 1
    low, high = jnp.where(odd, sine, cosine), jnp.where(odd, cosine, sine)
    cos_out = jnp.where(((index + 1) & 2) == 2, -low, low)
    sin_out = jnp.where((index & 2) == 2, -high, high)
    return cos_out, sin_out


def partial_kernel(kern_hbm, traces_hbm, out_hbm, kern, rows, part, sems):
    band = lax.axis_index("band")
    get_kern = pltpu.make_async_copy(kern_hbm.at[band], kern, sems.at[0])
    get_kern.start()
    gets, puts = [], []
    for q in range(PIECES):
        at = pl.ds(q * PIECE, PIECE)
        gets.append(pltpu.make_async_copy(traces_hbm.at[at], rows.at[at], sems.at[1 + q]))
        gets[q].start()
    get_kern.wait()
    for q in range(PIECES):
        gets[q].wait()
        piece = lax.dot_general(
            kern[...],
            rows[q * PIECE : (q + 1) * PIECE],
            NT_DIMS,
            preferred_element_type=jnp.float32,
        )
        lanes = pl.ds(q * PIECE // 2, PIECE // 2)
        for b in range(BANDS):
            block = piece[b * COLS : (b + 1) * COLS]
            part[b, :, q * PIECE // 2 : (q + 1) * PIECE // 2] = jnp.concatenate(
                [block[:, : PIECE // 2], block[:, PIECE // 2 :]], axis=0
            ).astype(jnp.bfloat16)
        puts.append(
            pltpu.make_async_copy(
                part.at[:, :, lanes], out_hbm.at[:, :, lanes], sems.at[1 + PIECES + q]
            )
        )
        puts[q].start()
    for put in puts:
        put.wait()


def signed_folded(shape, dim):
    index = lax.broadcasted_iota(jnp.int32, shape, dim)
    signed = jnp.where(index < HALF, index, jnp.where(index == HALF, -HALF, HALF - index))
    return signed.astype(jnp.float32) * (2.0 * math.pi / MIDS)


def slot_kernel(
    route_hbm, x_hbm, low_ref, high_ref, offset_ref, azimuth_ref, slot_ref, bins_ref, ints, sems
):
    copies = [
        pltpu.make_async_copy(route_hbm, ints.at[0], sems.at[0]),
        pltpu.make_async_copy(x_hbm, ints.at[1], sems.at[1]),
    ]
    for copy in copies:
        copy.start()
    block = MIDS
    row_i = lax.broadcasted_iota(jnp.int32, (block, block), 0)
    col_i = lax.broadcasted_iota(jnp.int32, (block, block), 1)
    upper = jnp.where(row_i < col_i, 1.0, 0.0).astype(jnp.bfloat16)
    class_i = lax.broadcasted_iota(jnp.int32, (CLASSES * TILES, block), 0)
    for i, ref in enumerate((low_ref, high_ref, offset_ref, azimuth_ref)):
        bins_ref[i] = jnp.full((8, 128), ref[0], jnp.int32)
    for copy in copies:
        copy.wait()
    cuts = [slice(step * block, (step + 1) * block) for step in range(ROWS // block)]
    members = []
    count = jnp.zeros((CLASSES * TILES, 1), jnp.float32)
    for cut in cuts:
        kind = (ints[1, :, cut] // WIDE) * TILES + ints[0, :, cut]
        members.append(jnp.where(class_i == kind, 1.0, 0.0))
        count = count + jnp.sum(members[-1], axis=1, keepdims=True)
    none = jnp.zeros((TILES, 1), jnp.float32)
    last = CAP - 1.0
    first = jnp.concatenate(
        [none, count[:TILES], last - count[3 * TILES :], none + last], axis=0
    )
    class_row = lax.broadcasted_iota(jnp.int32, (CLASSES * TILES, 1), 0)
    step_by = jnp.where(class_row < 2 * TILES, 1.0, -1.0)
    for cut, member in zip(cuts, members):
        earlier = jnp.dot(
            member.astype(jnp.bfloat16), upper, preferred_element_type=jnp.float32
        )
        slot = jnp.sum(member * (first + step_by * earlier), axis=0, keepdims=True)
        slot_ref[:, cut] = slot.astype(jnp.int32)
        first = first + step_by * jnp.sum(member, axis=1, keepdims=True)


def phase_kernel(bins_ref, sent_hbm, phase_ref):
    first = lax.axis_index("band") * F_DEV
    low, high, offset, azimuth = (bins_ref[i, :1, :1] for i in range(4))
    h = (offset.astype(jnp.float32) + 1.0) * 0.5
    cos_t, sin_t = sincos_turns(azimuth.astype(jnp.float32) * (0.5 / AZIMUTHS))
    kx = signed_folded((MIDS, MIDS), 0)
    ky = signed_folded((MIDS, MIDS), 1)
    inline = kx * (h * cos_t) + ky * (h * sin_t)
    along = signed_folded((MIDS, 128), 0) * h
    along = jnp.log1p(along * along)
    change = jnp.concatenate([along, along], axis=1) - jnp.log1p(inline * inline)
    unit = change * (0.5 / LOG_SPAN)
    turn_c, turn_s = sincos_turns(unit)
    cos_f, sin_f = sincos_turns(unit * (first + 1).astype(jnp.float32))
    scale = ROWS**-0.5 / MIDS
    for f in range(F_DEV):
        live = (first + f >= low) & (first + f < high)
        weight = jnp.where(live, scale, 0.0)
        phase_ref[0, f] = cos_f * weight
        phase_ref[1, f] = sin_f * weight
        if f + 1 < F_DEV:
            cos_f, sin_f = cos_f * turn_c - sin_f * turn_s, cos_f * turn_s + sin_f * turn_c


def place_kernel(
    part_hbm, rank_hbm, route_hbm, x_hbm, y_hbm, out_ref, part, ints, masked, sems
):
    copies = [
        pltpu.make_async_copy(src, ints.at[i], sems.at[i])
        for i, src in enumerate((rank_hbm, route_hbm, x_hbm, y_hbm))
    ]
    copies.append(pltpu.make_async_copy(part_hbm, part, sems.at[4]))
    for copy in copies:
        copy.start()
    for copy in copies[:4]:
        copy.wait()
    row = lax.broadcasted_iota(jnp.int32, (8, ROWS), 0)
    mids = jnp.where(
        row == 0,
        ints[2].astype(jnp.float32),
        jnp.where(row == 1, ints[3].astype(jnp.float32), jnp.where(row == 2, 1.0, 0.0)),
    )
    slot_i = lax.broadcasted_iota(jnp.int32, (CAP, ROWS), 0)
    slots = jnp.where(slot_i == ints[0], 1.0, 0.0).astype(jnp.bfloat16)
    tile = jnp.broadcast_to(ints[1], (16, ROWS))
    copies[4].wait()
    total = part[0].astype(jnp.float32)
    for b in range(1, BANDS):
        total = total + part[b].astype(jnp.float32)
    total = total.astype(jnp.bfloat16).astype(jnp.float32)
    lanes = [slice(q * PIECE // 2, (q + 1) * PIECE // 2) for q in range(PIECES)]
    spectra = jnp.concatenate(
        [total[h * COLS : (h + 1) * COLS, cut] for cut in lanes for h in range(2)], axis=1
    )
    values = jnp.concatenate([spectra, mids], axis=0)
    for g in range(TILES):
        masked[g * 16 : (g + 1) * 16, :] = jnp.where(tile == g, values, 0.0).astype(jnp.bfloat16)
    placed = lax.dot_general(masked[...], slots, NT_DIMS, preferred_element_type=jnp.float32)
    out_ref[...] = placed.astype(jnp.bfloat16).reshape(TILES, 16, CAP)


def tile_kernel(
    got_ref,
    table_hbm,
    tablet_hbm,
    phase_hbm,
    out_hbm,
    xa,
    xb,
    ya,
    yb,
    parts,
    cells,
    acc,
    table,
    tablet,
    phase,
    image,
    sems,
):
    copies = [
        pltpu.make_async_copy(table_hbm, table, sems.at[0]),
        pltpu.make_async_copy(tablet_hbm, tablet, sems.at[1]),
        pltpu.make_async_copy(phase_hbm, phase, sems.at[2]),
    ]
    for copy in copies:
        copy.start()
    lane_block = lax.broadcasted_iota(jnp.int32, (16, CAP), 1) // SPAN
    for i in range(TILES // PARTS):
        held = [got_ref[i * PARTS + k].astype(jnp.float32) for k in range(PARTS)]
        for d in (1, 2, 4):
            keep = (lane_block & d) == 0
            for k in range(PARTS):
                if k & d == 0:
                    a, b = held[k], held[k + d]
                    held[k] = jnp.where(keep, a, pltpu.roll(b, SPAN * d, 1))
                    held[k + d] = jnp.where(keep, pltpu.roll(a, CAP - SPAN * d, 1), b)
        for e in range(PARTS):
            parts[e, :, i * CAP : (i + 1) * CAP] = held[e].astype(jnp.bfloat16)
    parts[PARTS] = jnp.zeros((16, DEPTH), jnp.bfloat16)
    class_i = lax.broadcasted_iota(jnp.int32, (8, DEPTH), 0)
    bit_i = lax.broadcasted_iota(jnp.int32, (8, 1), 0)
    bits = jnp.zeros((8, 1), jnp.int32)
    for e in range(PARTS):
        tail = parts[e].astype(jnp.float32)
        kind = tail[COLS : COLS + 1].astype(jnp.int32) // WIDE
        hit = jnp.where((kind == class_i) & (tail[COLS + 2 : COLS + 3] > 0.5), 1.0, 0.0)
        found = jnp.max(hit, axis=1, keepdims=True).astype(jnp.int32)
        bits = bits + lax.shift_left(found, bit_i + CLASSES * e)
    mask = jnp.sum(jnp.where(bit_i < CLASSES, bits, 0))
    number = jnp.int32(0)
    for cell in range(PARTS * CLASSES):
        cells[number] = cell
        number = number + (lax.shift_right_logical(mask, jnp.int32(cell)) & 1)
    for extra in range(3):
        cells[number + extra] = PARTS * CLASSES

    iota = lax.broadcasted_iota(jnp.int32, (16, CAP), 0).astype(jnp.float32)
    one = jnp.ones((16, CAP), jnp.bfloat16)
    zero = jnp.zeros((16, CAP), jnp.bfloat16)

    def build(x_buf, y_buf, cell):
        part = cell // CLASSES
        start = ((cell % CLASSES) * WIDE).astype(jnp.float32)
        for i in range(DEPTH // CAP):
            cut = slice(i * CAP, (i + 1) * CAP)
            tail = parts[part, :, cut].astype(jnp.float32)
            rows = [
                jnp.broadcast_to(tail[c : c + 1], (16, CAP)).astype(jnp.bfloat16)
                for c in range(COLS + 2)
            ]
            for r in range(WIDE // 16):
                in_x = (iota + (start + 16.0 * r)).astype(jnp.bfloat16) == rows[COLS]
                for c in range(COLS):
                    at = c * WIDE + r * 16
                    x_buf[at : at + 16, cut] = jnp.where(in_x, rows[c], zero)
            for r in range(MIDS // 16):
                in_y = (iota + 16.0 * r).astype(jnp.bfloat16) == rows[COLS + 1]
                y_buf[r * 16 : (r + 1) * 16, cut] = jnp.where(in_y, one, zero)

    def add(x_buf, y_buf, cell):
        acc[cell % CLASSES] += lax.dot_general(
            x_buf[...], y_buf[...], NT_DIMS, preferred_element_type=jnp.float32
        )

    acc[...] = jnp.zeros_like(acc)
    build(xa, ya, cells[0])

    def pair(p, _):
        now, then, later = cells[2 * p], cells[2 * p + 1], cells[2 * p + 2]
        build(xb, yb, then)
        add(xa, ya, now)
        build(xa, ya, later)
        add(xb, yb, then)
        return 0

    lax.fori_loop(0, (number + 1) // 2, pair, 0)
    for copy in copies:
        copy.wait()

    lane0 = lax.broadcasted_iota(jnp.int32, (MIDS, HALF), 1) == 0
    bf = lambda v: v.astype(jnp.bfloat16)
    dot = lambda a, b: jnp.dot(a, b, preferred_element_type=jnp.float32)
    def stage_a(f):
        rows = [
            acc[q, c * WIDE : (c + 1) * WIDE]
            for c in (2 * f, 2 * f + 1)
            for q in range(CLASSES)
        ]
        u = dot(bf(jnp.concatenate(rows, axis=0)), table[...])
        cr, sr, ci, si = u[:MIDS, :HALF], u[:MIDS, HALF:], u[MIDS:, :HALF], u[MIDS:, HALF:]
        h_r = [jnp.where(lane0, cr, cr + si), jnp.where(lane0, sr, cr - si)]
        h_i = [jnp.where(lane0, ci, ci - sr), jnp.where(lane0, si, ci + sr)]
        return bf(jnp.concatenate(h_r + h_i, axis=1))

    top0 = lax.broadcasted_iota(jnp.int32, (8, MIDS), 0) == 0

    def pick_row0(zero_row, rest):
        return jnp.concatenate([jnp.where(top0, zero_row[:8], rest[:8]), rest[8:]], axis=0)

    def stage_b(f, h):
        v = dot(tablet[...], h)
        cr, sr, ci, si = v[:HALF, :MIDS], v[HALF:, :MIDS], v[:HALF, MIDS:], v[HALF:, MIDS:]
        wpr, wpi = pick_row0(cr, cr + si), pick_row0(ci, ci - sr)
        wmr, wmi = pick_row0(sr, cr - si), pick_row0(si, ci + sr)
        pc, ps = phase[0, f, :HALF], phase[1, f, :HALF]
        mc, ms = phase[0, f, HALF:], phase[1, f, HALF:]
        mpr, mpi = wpr * pc - wpi * ps, wpr * ps + wpi * pc
        mmr, mmi = wmr * mc - wmi * ms, wmr * ms + wmi * mc
        a_r, a_i = pick_row0(mpr, mpr + mmr), pick_row0(mpi, mpi + mmi)
        d_r, d_i = pick_row0(mmr, mmi - mpi), pick_row0(mmi, mpr - mmr)
        return bf(
            jnp.concatenate(
                [jnp.concatenate([a_r, a_i], axis=1), jnp.concatenate([d_r, d_i], axis=1)],
                axis=0,
            )
        )

    def stage_c(f, folded):
        q = dot(table[...], folded)
        qpr, qmr = q[:, :HALF], q[:, HALF:MIDS]
        qpi, qmi = q[:, MIDS : MIDS + HALF], q[:, MIDS + HALF :]
        a_r = jnp.where(lane0, qpr, qpr + qmr)
        a_i = jnp.where(lane0, qpi, qpi + qmi)
        d_r = jnp.where(lane0, qmr, qmi - qpi)
        d_i = jnp.where(lane0, qmi, qpr - qmr)
        return bf(
            jnp.concatenate(
                [jnp.concatenate([a_r, d_r], axis=1), jnp.concatenate([a_i, d_i], axis=1)],
                axis=0,
            )
        )

    def stage_d(f, folded):
        w = dot(folded, tablet[...])
        image[f, :, :MIDS] = w[:MIDS]
        image[f, :, MIDS:] = w[MIDS:]
        put = pltpu.make_async_copy(image.at[f], out_hbm.at[f], sems.at[3 + f])
        put.start()
        puts.append(put)

    puts = []
    stages = (stage_b, stage_c, stage_d)
    held = {}
    for step in range(F_DEV + 3):
        for f in range(F_DEV):
            if f == step:
                held[f] = stage_a(f)
            elif 0 < step - f <= 3:
                held[f] = stages[step - f - 1](f, held[f])
    for put in puts:
        put.wait()


VM = pl.BlockSpec(memory_space=pltpu.VMEM)
SM = pl.BlockSpec(memory_space=pltpu.SMEM)
ANY = pl.BlockSpec(memory_space=pl.ANY)


def vmem(mib):
    return pltpu.CompilerParams(vmem_limit_bytes=mib * 1024 * 1024)


def cost(flops, moved):
    return pl.CostEstimate(flops=flops, bytes_accessed=moved, transcendentals=0)


def partial_spectra(kern, traces):
    return pl.pallas_call(
        partial_kernel,
        out_shape=jax.ShapeDtypeStruct((BANDS, 16, ROWS // 2), jnp.bfloat16),
        in_specs=[ANY, ANY],
        out_specs=ANY,
        scratch_shapes=[
            pltpu.VMEM((COLS * BANDS, SAMPLES), jnp.bfloat16),
            pltpu.VMEM((ROWS, SAMPLES), jnp.bfloat16),
            pltpu.VMEM((BANDS, 16, ROWS // 2), jnp.bfloat16),
            pltpu.SemaphoreType.DMA((1 + 2 * PIECES,)),
        ],
        compiler_params=vmem(60),
        cost_estimate=cost(2 * 64 * SAMPLES * ROWS, 800_000),
        name="partial_spectra",
    )(kern, traces)


def slot_ranks(route, mid_x, low, high, offset, azimuth):
    return pl.pallas_call(
        slot_kernel,
        out_shape=(
            jax.ShapeDtypeStruct((1, ROWS), jnp.int32),
            jax.ShapeDtypeStruct((4, 8, 128), jnp.int32),
        ),
        in_specs=[ANY] * 2 + [SM] * 4,
        out_specs=(VM, VM),
        scratch_shapes=[pltpu.VMEM((2, 1, ROWS), jnp.int32), pltpu.SemaphoreType.DMA((2,))],
        compiler_params=vmem(8),
        cost_estimate=cost(2_000_000_000, 3_000_000),
        name="slot_ranks",
    )(route, mid_x, low, high, offset, azimuth)


def phase_table(bins, sent):
    return pl.pallas_call(
        phase_kernel,
        out_shape=jax.ShapeDtypeStruct((2, F_DEV, MIDS, MIDS), jnp.float32),
        in_specs=[VM, ANY],
        out_specs=VM,
        compiler_params=vmem(16),
        cost_estimate=cost(2_000_000_000, 3_000_000),
        name="phase_table",
    )(bins, sent)


def place(part, rank, route, mid_x, mid_y):
    return pl.pallas_call(
        place_kernel,
        out_shape=jax.ShapeDtypeStruct((TILES, 16, CAP), jnp.bfloat16),
        in_specs=[ANY] * 5,
        out_specs=VM,
        scratch_shapes=[
            pltpu.VMEM((BANDS, 16, ROWS // 2), jnp.bfloat16),
            pltpu.VMEM((4, 1, ROWS), jnp.int32),
            pltpu.VMEM((TILES * 16, ROWS), jnp.bfloat16),
            pltpu.SemaphoreType.DMA((5,)),
        ],
        compiler_params=vmem(16),
        cost_estimate=cost(2 * 512 * ROWS * CAP, 1_000_000),
        name="place",
    )(part, rank, route, mid_x, mid_y)


def tile_image(got, table, tablet, phase):
    return pl.pallas_call(
        tile_kernel,
        out_shape=jax.ShapeDtypeStruct((F_DEV, MIDS, 2 * MIDS), jnp.float32),
        in_specs=[VM, ANY, ANY, ANY],
        out_specs=ANY,
        scratch_shapes=[
            pltpu.VMEM((COLS * WIDE, DEPTH), jnp.bfloat16),
            pltpu.VMEM((COLS * WIDE, DEPTH), jnp.bfloat16),
            pltpu.VMEM((MIDS, DEPTH), jnp.bfloat16),
            pltpu.VMEM((MIDS, DEPTH), jnp.bfloat16),
            pltpu.VMEM((PARTS + 1, 16, DEPTH), jnp.bfloat16),
            pltpu.SMEM((PARTS * CLASSES + 8,), jnp.int32),
            pltpu.VMEM((CLASSES, COLS * WIDE, MIDS), jnp.float32),
            pltpu.VMEM((MIDS, MIDS), jnp.bfloat16),
            pltpu.VMEM((MIDS, MIDS), jnp.bfloat16),
            pltpu.VMEM((2, F_DEV, MIDS, MIDS), jnp.float32),
            pltpu.VMEM((F_DEV, MIDS, 2 * MIDS), jnp.float32),
            pltpu.SemaphoreType.DMA((3 + F_DEV,)),
        ],
        compiler_params=vmem(32),
        cost_estimate=cost(6_000_000_000, 5_000_000),
        name="tile_image",
    )(got, table, tablet, phase)


def per_device(traces, route, mid_x, mid_y, band_low, band_high, offset_bin, azimuth_bin):
    table = folded_table()
    route = route.reshape(1, ROWS)
    mid_x = mid_x.reshape(1, ROWS)
    mid_y = mid_y.reshape(1, ROWS)
    part = partial_spectra(jnp.asarray(time_kernel_blocks()), traces)
    part = lax.all_to_all(part, "band", split_axis=0, concat_axis=0, tiled=True)
    rank, bins = slot_ranks(route, mid_x, band_low, band_high, offset_bin, azimuth_bin)
    sent = place(part, rank, route, mid_x, mid_y)
    got = lax.all_to_all(sent, "tile", split_axis=0, concat_axis=0, tiled=True)
    phase = phase_table(bins, sent)
    image = tile_image(got, jnp.asarray(table), jnp.asarray(np.ascontiguousarray(table.T)), phase)
    return image[None]


def solution(mesh):
    return jax.shard_map(
        per_device,
        mesh=mesh,
        in_specs=(
            P("tile", "band"),
            P("tile", None),
            P("tile"),
            P("tile"),
            P("tile"),
            P("tile"),
            P("tile"),
            P("tile"),
        ),
        out_specs=P("tile", "band", None, None),
        check_vma=False,
    )
```

time: 50.5 us -> 44.8 us (0.89)
  the two profiles are of different devices: /device:TPU:8 before, /device:TPU:32 now
where the time goes in v2:
time: 44.8 us; the launch traced here: 44.2 us
  starting transfers between devices  15.7 us (35%)
  Pallas kernels  13.6 us (30%)
  waiting for transfers between devices  10.9 us (24%)
  between operations  2.67 us (6%)
  local copies, waits for them, and re-layouts  1.41 us (3%)
    all_to_all x1, starting transfers between devices, per_device(): got = lax.all_to_all(sent, 'tile', split_axis=0, concat_axis=0, tiled=True)  11.2 us
    all_to_all x1, waiting for transfers between devices, per_device(): got = lax.all_to_all(sent, 'tile', split_axis=0, concat_axis=0, tiled=True)  7.92 us
    pallas_call x1, Pallas kernels, tile_image(): pl.pallas_call(tile_kernel, out_shape=jax.ShapeDtypeStruct((F_DEV, MIDS,...  7.54 us
    all_to_all x1, starting transfers between devices, per_device(): part = lax.all_to_all(part, 'band', split_axis=0, concat_axis=0, tiled=True)  4.47 us
    all_to_all x1, waiting for transfers between devices, per_device(): part = lax.all_to_all(part, 'band', split_axis=0, concat_axis=0, tiled=True)  2.96 us
    pallas_call x1, Pallas kernels, partial_spectra(): pl.pallas_call(partial_kernel, out_shape=jax.ShapeDtypeStruct((BANDS, 16,...  2.09 us
    pallas_call x1, Pallas kernels, phase_table(): pl.pallas_call(phase_kernel, out_shape=jax.ShapeDtypeStruct((2, F_DEV, MI...  1.73 us
    pallas_call x1, Pallas kernels, place(): pl.pallas_call(place_kernel, out_shape=jax.ShapeDtypeStruct((TILES, 16, C...  1.63 us
  transfers between devices with their start and end apart: 2, of which 2 were waited for; matrix products, arithmetic and copies ran while one was open for 0% of the time, Pallas kernels for 5%

profile of v2, /device:TPU:32, one launch (start us, length us, event | category | flops | bytes accessed | tf_op | source)
XLA Modules:
  0.0 44.2 jit_solution(11602862499328439750)
XLA Ops:
  0.0 2.1 %partial_spectra.1 = bf16[8,16,1024]{2,1,0:T(8,128)(2,1)} custom-call(bf16[8,64,128]{2,1,0:T(8,128)(2,1)} %constant.6.clone.kern_hbm, bf16[2048,128]{1,0:T(8,128)(2,1)} %traces_hbm.1), custom_call_target="tpu_custom_call" | custom-call | flops 33554432 | bytes 800000 | tf_op jit(solution)/shard_map/partial_spectra/pallas_call | solution.py:398
  2.1 4.5 %all-to-all-start = ((bf16[8,16,1024]{2,1,0:T(8,128)(2,1)}), bf16[8,16,1024]{2,1,0:T(8,128)(2,1)S(1)}, u32[]{:S(2)}, u32[]{:S(2)}) async-start(bf16[8,16,1024]{2,1,0:T(8,128)(2,1)} %partial_spectra.1), calls=%async_computation | async-start | bytes 524288 | tf_op jit(solution)/shard_map/all_to_all | solution.py:493
  9.2 0.0 copy-start
  9.2 0.7 %copy-done = s32[2048,1]{0,1:T(1,128)S(1)} copy-done((s32[2048,1]{0,1:T(1,128)S(1)}, s32[2048,1]{0,1:T(1,128)}, u32[]{:S(2)}) %copy-start) | copy-done | bytes 8216
  9.9 0.0 copy-start.2
  9.9 0.7 %copy-done.2 = s32[2048]{0:T(1024)S(1)} copy-done((s32[2048]{0:T(1024)S(1)}, s32[2048]{0:T(1024)}, u32[]{:S(2)}) %copy-start.2) | copy-done | bytes 8216
  10.6 0.0 copy-start.1
  10.6 0.0 copy-start.3
  10.6 0.0 copy-start.4
  10.6 0.6 %slot_ranks.1 = (s32[1,2048]{1,0:T(1,128)S(1)}, s32[4,8,128]{2,1,0:T(8,128)S(1)}) custom-call(s32[1,2048]{1,0:T(1,128)S(1)} %bitcast.4, s32[1,2048]{1,0:T(1,128)S(1)} %bitcast.6, s32[1]{0:T(128)S(6)} %copy.12.low_ref, s32[1]{0:T(128)S(6)} %copy.13.high_ref, s32[1]{0:T(128)S(6)} %copy.14.offset_ref, s32[1]{0:T(128)S(6)} %copy.15.azimuth_ref), custom_call_target="tpu_custom_call" | custom-call | flops 2000000000 | bytes 3000000 | tf_op jit(solution)/shard_map/slot_ranks/pallas_call | solution.py:416
  11.2 3.0 %all-to-all-done.part_hbm = bf16[8,16,1024]{2,1,0:T(8,128)(2,1)S(1)} async-done(((bf16[8,16,1024]{2,1,0:T(8,128)(2,1)}), bf16[8,16,1024]{2,1,0:T(8,128)(2,1)S(1)}, u32[]{:S(2)}, u32[]{:S(2)}) %all-to-all-start) | async-done | bytes 262176 | tf_op jit(solution)/shard_map/all_to_all | solution.py:493
  14.1 0.0 copy-done.1
  14.1 0.0 copy-done.3
  14.1 0.0 copy-done.4
  14.1 1.6 %place.1.sent_hbm = bf16[32,16,128]{2,1,0:T(8,128)(2,1)} custom-call(bf16[8,16,1024]{2,1,0:T(8,128)(2,1)S(1)} %all-to-all-done.part_hbm, s32[1,2048]{1,0:T(1,128)S(1)} %get-tuple-element.7.rank_hbm, s32[1,2048]{1,0:T(1,128)S(1)} %bitcast.5, s32[1,2048]{1,0:T(1,128)S(1)} %bitcast.7, s32[1,2048]{1,0:T(1,128)S(1)} %bitcast.8), custom_call_target="tpu_custom_call" | custom-call | flops 268435456 | bytes 1000000 | tf_op jit(solution)/shard_map/place/pallas_call | solution.py:444
  15.8 11.2 %all-to-all-start.1 = ((bf16[32,16,128]{2,1,0:T(8,128)(2,1)}), bf16[32,16,128]{2,1,0:T(8,128)(2,1)S(1)}, u32[]{:S(2)}, u32[]{:S(2)}) async-start(bf16[32,16,128]{2,1,0:T(8,128)(2,1)} %place.1.sent_hbm), calls=%async_computation.1 | async-start | bytes 262144 | tf_op jit(solution)/shard_map/all_to_all | solution.py:496
  27.0 0.0 copy-start.5
  27.0 0.0 copy-start.6
  27.0 1.7 %phase_table.1.phase_hbm = f32[2,4,256,256]{3,2,1,0:T(8,128)S(1)} custom-call(s32[4,8,128]{2,1,0:T(8,128)S(1)} %get-tuple-element.8.bins_ref, bf16[32,16,128]{2,1,0:T(8,128)(2,1)} %place.1.sent_hbm), custom_call_target="tpu_custom_call" | custom-call | flops 2000000000 | bytes 3000000 | tf_op jit(solution)/shard_map/phase_table/pallas_call | solution.py:432
  28.7 7.9 %all-to-all-done.1.got_ref = bf16[32,16,128]{2,1,0:T(8,128)(2,1)S(1)} async-done(((bf16[32,16,128]{2,1,0:T(8,128)(2,1)}), bf16[32,16,128]{2,1,0:T(8,128)(2,1)S(1)}, u32[]{:S(2)}, u32[]{:S(2)}) %all-to-all-start.1) | async-done | bytes 131104 | tf_op jit(solution)/shard_map/all_to_all | solution.py:496
  36.7 0.0 copy-done.5
  36.7 0.0 copy-done.6
  36.7 7.5 %tile_image.1 = f32[4,256,512]{2,1,0:T(8,128)} custom-call(bf16[32,16,128]{2,1,0:T(8,128)(2,1)S(1)} %all-to-all-done.1.got_ref, bf16[256,256]{1,0:T(8,128)(2,1)S(1)} %copy-done.6, bf16[256,256]{1,0:T(8,128)(2,1)S(1)} %copy-done.5, f32[2,4,256,256]{3,2,1,0:T(8,128)S(1)} %phase_table.1.phase_hbm), custom_call_target="tpu_custom_call" | custom-call | flops 6000000000 | bytes 5000000 | tf_op jit(solution)/shard_map/tile_image/pallas_call | solution.py:462
Async XLA Ops:
  2.1 12.0 %all-to-all-start = ((bf16[8,16,1024]{2,1,0:T(8,128)(2,1)}), bf16[8,16,1024]{2,1,0:T(8,128)(2,1)S(1)}, u32[]{:S(2)}, u32[]{:S(2)}) async-start(bf16[8,16,1024]{2,1,0:T(8,128)(2,1)} %partial_spectra.1), calls=%async_computation | async-start | bytes 524288 | tf_op jit(solution)/shard_map/all_to_all | solution.py:493
  9.2 0.7 %copy-start = (s32[2048,1]{0,1:T(1,128)S(1)}, s32[2048,1]{0,1:T(1,128)}, u32[]{:S(2)}) copy-start(s32[2048,1]{0,1:T(1,128)} %param.12) | copy-start | bytes 24580
  9.9 0.7 %copy-start.2 = (s32[2048]{0:T(1024)S(1)}, s32[2048]{0:T(1024)}, u32[]{:S(2)}) copy-start(s32[2048]{0:T(1024)} %param.13) | copy-start | bytes 24580
  10.6 3.6 %copy-start.1 = (s32[2048,1]{0,1:T(1,128)S(1)}, s32[2048,1]{0,1:T(1,128)}, u32[]{:S(2)}) copy-start(s32[2048,1]{0,1:T(1,128)} %param.12) | copy-start | bytes 24580
  10.6 3.6 %copy-start.3 = (s32[2048]{0:T(1024)S(1)}, s32[2048]{0:T(1024)}, u32[]{:S(2)}) copy-start(s32[2048]{0:T(1024)} %param.13) | copy-start | bytes 24580
  10.6 3.6 %copy-start.4 = (s32[2048]{0:T(1024)S(1)}, s32[2048]{0:T(1024)}, u32[]{:S(2)}) copy-start(s32[2048]{0:T(1024)} %param.14) | copy-start | bytes 24580
  15.8 20.9 %all-to-all-start.1 = ((bf16[32,16,128]{2,1,0:T(8,128)(2,1)}), bf16[32,16,128]{2,1,0:T(8,128)(2,1)S(1)}, u32[]{:S(2)}, u32[]{:S(2)}) async-start(bf16[32,16,128]{2,1,0:T(8,128)(2,1)} %place.1.sent_hbm), calls=%async_computation.1 | async-start | bytes 262144 | tf_op jit(solution)/shard_map/all_to_all | solution.py:496
  27.0 9.7 %copy-start.5 = (bf16[256,256]{1,0:T(8,128)(2,1)S(1)}, bf16[256,256]{1,0:T(8,128)(2,1)}, u32[]{:S(2)}) copy-start(bf16[256,256]{1,0:T(8,128)(2,1)} %constant.8.clone.tablet_hbm) | copy-start | bytes 393220
  27.0 9.7 %copy-start.6 = (bf16[256,256]{1,0:T(8,128)(2,1)S(1)}, bf16[256,256]{1,0:T(8,128)(2,1)}, u32[]{:S(2)}) copy-start(bf16[256,256]{1,0:T(8,128)(2,1)} %constant.7.clone.table_hbm) | copy-start | bytes 393220

commit v3 on v2

--- a/solution.py
+++ b/solution.py
@@ -26,6 +26,7 @@
 PARTS = 8
 SPAN = CAP // PARTS
 DEPTH = TILES * SPAN
+UNROLL = 16
 PIECES = 1
 PIECE = ROWS // PIECES
 NT_DIMS = (((1,), (1,)), ((), ()))
@@ -171,31 +172,19 @@
             cos_f, sin_f = cos_f * turn_c - sin_f * turn_s, cos_f * turn_s + sin_f * turn_c
 
 
-def place_kernel(
-    part_hbm, rank_hbm, route_hbm, x_hbm, y_hbm, out_ref, part, ints, masked, sems
-):
-    copies = [
-        pltpu.make_async_copy(src, ints.at[i], sems.at[i])
-        for i, src in enumerate((rank_hbm, route_hbm, x_hbm, y_hbm))
-    ]
-    copies.append(pltpu.make_async_copy(part_hbm, part, sems.at[4]))
-    for copy in copies:
-        copy.start()
-    for copy in copies[:4]:
-        copy.wait()
+def place_kernel(part_ref, rank_ref, route_ref, x_ref, y_ref, out_ref, masked):
     row = lax.broadcasted_iota(jnp.int32, (8, ROWS), 0)
     mids = jnp.where(
         row == 0,
-        ints[2].astype(jnp.float32),
-        jnp.where(row == 1, ints[3].astype(jnp.float32), jnp.where(row == 2, 1.0, 0.0)),
+        x_ref[...].astype(jnp.float32),
+        jnp.where(row == 1, y_ref[...].astype(jnp.float32), jnp.where(row == 2, 1.0, 0.0)),
     )
     slot_i = lax.broadcasted_iota(jnp.int32, (CAP, ROWS), 0)
-    slots = jnp.where(slot_i == ints[0], 1.0, 0.0).astype(jnp.bfloat16)
-    tile = jnp.broadcast_to(ints[1], (16, ROWS))
-    copies[4].wait()
-    total = part[0].astype(jnp.float32)
+    slots = jnp.where(slot_i == rank_ref[...], 1.0, 0.0).astype(jnp.bfloat16)
+    tile = jnp.broadcast_to(route_ref[...], (16, ROWS))
+    total = part_ref[0].astype(jnp.float32)
     for b in range(1, BANDS):
-        total = total + part[b].astype(jnp.float32)
+        total = total + part_ref[b].astype(jnp.float32)
     total = total.astype(jnp.bfloat16).astype(jnp.float32)
     lanes = [slice(q * PIECE // 2, (q + 1) * PIECE // 2) for q in range(PIECES)]
     spectra = jnp.concatenate(
@@ -261,7 +250,7 @@
     for cell in range(PARTS * CLASSES):
         cells[number] = cell
         number = number + (lax.shift_right_logical(mask, jnp.int32(cell)) & 1)
-    for extra in range(3):
+    for extra in range(UNROLL + 1):
         cells[number + extra] = PARTS * CLASSES
 
     iota = lax.broadcasted_iota(jnp.int32, (16, CAP), 0).astype(jnp.float32)
@@ -295,15 +284,14 @@
     acc[...] = jnp.zeros_like(acc)
     build(xa, ya, cells[0])
 
-    def pair(p, _):
-        now, then, later = cells[2 * p], cells[2 * p + 1], cells[2 * p + 2]
-        build(xb, yb, then)
-        add(xa, ya, now)
-        build(xa, ya, later)
-        add(xb, yb, then)
+    def many(p, _):
+        for k in range(UNROLL):
+            here, there = ((xa, ya), (xb, yb))[:: 1 if k % 2 == 0 else -1]
+            build(*there, cells[UNROLL * p + k + 1])
+            add(*here, cells[UNROLL * p + k])
         return 0
 
-    lax.fori_loop(0, (number + 1) // 2, pair, 0)
+    lax.fori_loop(0, (number + UNROLL - 1) // UNROLL, many, 0)
     for copy in copies:
         copy.wait()
 
@@ -361,22 +349,25 @@
         )
 
     def stage_d(f, folded):
-        w = dot(folded, tablet[...])
-        image[f, :, :MIDS] = w[:MIDS]
-        image[f, :, MIDS:] = w[MIDS:]
-        put = pltpu.make_async_copy(image.at[f], out_hbm.at[f], sems.at[3 + f])
-        put.start()
-        puts.append(put)
+        for i in range(2):
+            cut = slice(i * MIDS, (i + 1) * MIDS)
+            image[f, :, cut] = dot(folded[cut], tablet[...])
+            put = pltpu.make_async_copy(
+                image.at[f, :, cut], out_hbm.at[f, :, cut], sems.at[3 + 2 * f + i]
+            )
+            put.start()
+            puts.append(put)
 
     puts = []
     stages = (stage_b, stage_c, stage_d)
     held = {}
-    for step in range(F_DEV + 3):
-        for f in range(F_DEV):
-            if f == step:
-                held[f] = stage_a(f)
-            elif 0 < step - f <= 3:
-                held[f] = stages[step - f - 1](f, held[f])
+    for step in range(5):
+        for g in range(2):
+            for f in (2 * g, 2 * g + 1):
+                if g == step:
+                    held[f] = stage_a(f)
+                elif 0 < step - g <= 3:
+                    held[f] = stages[step - g - 1](f, held[f])
     for put in puts:
         put.wait()
 
@@ -444,13 +435,10 @@
     return pl.pallas_call(
         place_kernel,
         out_shape=jax.ShapeDtypeStruct((TILES, 16, CAP), jnp.bfloat16),
-        in_specs=[ANY] * 5,
+        in_specs=[VM] * 5,
         out_specs=VM,
         scratch_shapes=[
-            pltpu.VMEM((BANDS, 16, ROWS // 2), jnp.bfloat16),
-            pltpu.VMEM((4, 1, ROWS), jnp.int32),
             pltpu.VMEM((TILES * 16, ROWS), jnp.bfloat16),
-            pltpu.SemaphoreType.DMA((5,)),
         ],
         compiler_params=vmem(16),
         cost_estimate=cost(2 * 512 * ROWS * CAP, 1_000_000),
@@ -470,13 +458,13 @@
             pltpu.VMEM((MIDS, DEPTH), jnp.bfloat16),
             pltpu.VMEM((MIDS, DEPTH), jnp.bfloat16),
             pltpu.VMEM((PARTS + 1, 16, DEPTH), jnp.bfloat16),
-            pltpu.SMEM((PARTS * CLASSES + 8,), jnp.int32),
+            pltpu.SMEM((PARTS * CLASSES + UNROLL + 2,), jnp.int32),
             pltpu.VMEM((CLASSES, COLS * WIDE, MIDS), jnp.float32),
             pltpu.VMEM((MIDS, MIDS), jnp.bfloat16),
             pltpu.VMEM((MIDS, MIDS), jnp.bfloat16),
             pltpu.VMEM((2, F_DEV, MIDS, MIDS), jnp.float32),
             pltpu.VMEM((F_DEV, MIDS, 2 * MIDS), jnp.float32),
-            pltpu.SemaphoreType.DMA((3 + F_DEV,)),
+            pltpu.SemaphoreType.DMA((3 + 2 * F_DEV,)),
         ],
         compiler_params=vmem(32),
         cost_estimate=cost(6_000_000_000, 5_000_000),

time: 44.8 us -> 44.5 us (level)
  no operation moved by 1% of the time
where the time goes in v3:
time: 44.5 us; the launch traced here: 43.9 us
  starting transfers between devices  15.7 us (35%)
  Pallas kernels  13.3 us (30%)
  waiting for transfers between devices  10.9 us (24%)
  between operations  2.66 us (6%)
  local copies, waits for them, and re-layouts  1.41 us (3%)
    all_to_all x1, starting transfers between devices, per_device(): got = lax.all_to_all(sent, 'tile', split_axis=0, concat_axis=0, tiled=True)  11.2 us
    all_to_all x1, waiting for transfers between devices, per_device(): got = lax.all_to_all(sent, 'tile', split_axis=0, concat_axis=0, tiled=True)  7.92 us
    pallas_call x1, Pallas kernels, tile_image(): pl.pallas_call(tile_kernel, out_shape=jax.ShapeDtypeStruct((F_DEV, MIDS,...  7.53 us
    all_to_all x1, starting transfers between devices, per_device(): part = lax.all_to_all(part, 'band', split_axis=0, concat_axis=0, tiled=True)  4.47 us
    all_to_all x1, waiting for transfers between devices, per_device(): part = lax.all_to_all(part, 'band', split_axis=0, concat_axis=0, tiled=True)  2.96 us
    pallas_call x1, Pallas kernels, partial_spectra(): pl.pallas_call(partial_kernel, out_shape=jax.ShapeDtypeStruct((BANDS, 16,...  2.09 us
    pallas_call x1, Pallas kernels, phase_table(): pl.pallas_call(phase_kernel, out_shape=jax.ShapeDtypeStruct((2, F_DEV, MI...  1.73 us
    unnamed x14, local copies, waits for them, and re-layouts  1.41 us
  transfers between devices with their start and end apart: 2, of which 2 were waited for; matrix products, arithmetic and copies ran while one was open for 0% of the time, Pallas kernels for 5%

profile of v3, /device:TPU:32, one launch (start us, length us, event | category | flops | bytes accessed | tf_op | source)
XLA Modules:
  0.0 43.9 jit_solution(12615845070932683275)
XLA Ops:
  0.0 2.1 %partial_spectra.1 = bf16[8,16,1024]{2,1,0:T(8,128)(2,1)} custom-call(bf16[8,64,128]{2,1,0:T(8,128)(2,1)} %constant.6.clone.kern_hbm, bf16[2048,128]{1,0:T(8,128)(2,1)} %traces_hbm.1), custom_call_target="tpu_custom_call" | custom-call | flops 33554432 | bytes 800000 | tf_op jit(solution)/shard_map/partial_spectra/pallas_call | solution.py:389
  2.1 4.5 %all-to-all-start = ((bf16[8,16,1024]{2,1,0:T(8,128)(2,1)}), bf16[8,16,1024]{2,1,0:T(8,128)(2,1)S(1)}, u32[]{:S(2)}, u32[]{:S(2)}) async-start(bf16[8,16,1024]{2,1,0:T(8,128)(2,1)} %partial_spectra.1), calls=%async_computation | async-start | bytes 524288 | tf_op jit(solution)/shard_map/all_to_all | solution.py:481
  9.2 0.0 copy-start
  9.2 0.7 %copy-done = s32[2048,1]{0,1:T(1,128)S(1)} copy-done((s32[2048,1]{0,1:T(1,128)S(1)}, s32[2048,1]{0,1:T(1,128)}, u32[]{:S(2)}) %copy-start) | copy-done | bytes 8216
  9.9 0.0 copy-start.2
  9.9 0.7 %copy-done.2 = s32[2048]{0:T(1024)S(1)} copy-done((s32[2048]{0:T(1024)S(1)}, s32[2048]{0:T(1024)}, u32[]{:S(2)}) %copy-start.2) | copy-done | bytes 8216
  10.6 0.0 copy-start.1
  10.6 0.0 copy-start.3
  10.6 0.0 copy-start.4
  10.6 0.6 %slot_ranks.1 = (s32[1,2048]{1,0:T(1,128)S(1)}, s32[4,8,128]{2,1,0:T(8,128)S(1)}) custom-call(s32[1,2048]{1,0:T(1,128)S(1)} %bitcast.4, s32[1,2048]{1,0:T(1,128)S(1)} %bitcast.6, s32[1]{0:T(128)S(6)} %copy.12.low_ref, s32[1]{0:T(128)S(6)} %copy.13.high_ref, s32[1]{0:T(128)S(6)} %copy.14.offset_ref, s32[1]{0:T(128)S(6)} %copy.15.azimuth_ref), custom_call_target="tpu_custom_call" | custom-call | flops 2000000000 | bytes 3000000 | tf_op jit(solution)/shard_map/slot_ranks/pallas_call | solution.py:407
  11.2 3.0 %all-to-all-done.part_ref = bf16[8,16,1024]{2,1,0:T(8,128)(2,1)S(1)} async-done(((bf16[8,16,1024]{2,1,0:T(8,128)(2,1)}), bf16[8,16,1024]{2,1,0:T(8,128)(2,1)S(1)}, u32[]{:S(2)}, u32[]{:S(2)}) %all-to-all-start) | async-done | bytes 262176 | tf_op jit(solution)/shard_map/all_to_all | solution.py:481
  14.1 0.0 copy-done.1
  14.1 0.0 copy-done.3
  14.1 0.0 copy-done.4
  14.1 1.4 %place.1.sent_hbm = bf16[32,16,128]{2,1,0:T(8,128)(2,1)} custom-call(bf16[8,16,1024]{2,1,0:T(8,128)(2,1)S(1)} %all-to-all-done.part_ref, s32[1,2048]{1,0:T(1,128)S(1)} %get-tuple-element.7.rank_ref, s32[1,2048]{1,0:T(1,128)S(1)} %bitcast.5, s32[1,2048]{1,0:T(1,128)S(1)} %bitcast.7, s32[1,2048]{1,0:T(1,128)S(1)} %bitcast.8), custom_call_target="tpu_custom_call" | custom-call | flops 268435456 | bytes 1000000 | tf_op jit(solution)/shard_map/place/pallas_call | solution.py:435
  15.5 11.2 %all-to-all-start.1 = ((bf16[32,16,128]{2,1,0:T(8,128)(2,1)}), bf16[32,16,128]{2,1,0:T(8,128)(2,1)S(1)}, u32[]{:S(2)}, u32[]{:S(2)}) async-start(bf16[32,16,128]{2,1,0:T(8,128)(2,1)} %place.1.sent_hbm), calls=%async_computation.1 | async-start | bytes 262144 | tf_op jit(solution)/shard_map/all_to_all | solution.py:484
  26.7 0.0 copy-start.5
  26.7 0.0 copy-start.6
  26.7 1.7 %phase_table.1.phase_hbm = f32[2,4,256,256]{3,2,1,0:T(8,128)S(1)} custom-call(s32[4,8,128]{2,1,0:T(8,128)S(1)} %get-tuple-element.8.bins_ref, bf16[32,16,128]{2,1,0:T(8,128)(2,1)} %place.1.sent_hbm), custom_call_target="tpu_custom_call" | custom-call | flops 2000000000 | bytes 3000000 | tf_op jit(solution)/shard_map/phase_table/pallas_call | solution.py:423
  28.5 7.9 %all-to-all-done.1.got_ref = bf16[32,16,128]{2,1,0:T(8,128)(2,1)S(1)} async-done(((bf16[32,16,128]{2,1,0:T(8,128)(2,1)}), bf16[32,16,128]{2,1,0:T(8,128)(2,1)S(1)}, u32[]{:S(2)}, u32[]{:S(2)}) %all-to-all-start.1) | async-done | bytes 131104 | tf_op jit(solution)/shard_map/all_to_all | solution.py:484
  36.4 0.0 copy-done.5
  36.4 0.0 copy-done.6
  36.4 7.5 %tile_image.1 = f32[4,256,512]{2,1,0:T(8,128)} custom-call(bf16[32,16,128]{2,1,0:T(8,128)(2,1)S(1)} %all-to-all-done.1.got_ref, bf16[256,256]{1,0:T(8,128)(2,1)S(1)} %copy-done.6, bf16[256,256]{1,0:T(8,128)(2,1)S(1)} %copy-done.5, f32[2,4,256,256]{3,2,1,0:T(8,128)S(1)} %phase_table.1.phase_hbm), custom_call_target="tpu_custom_call" | custom-call | flops 6000000000 | bytes 5000000 | tf_op jit(solution)/shard_map/tile_image/pallas_call | solution.py:450
Async XLA Ops:
  2.1 12.0 %all-to-all-start = ((bf16[8,16,1024]{2,1,0:T(8,128)(2,1)}), bf16[8,16,1024]{2,1,0:T(8,128)(2,1)S(1)}, u32[]{:S(2)}, u32[]{:S(2)}) async-start(bf16[8,16,1024]{2,1,0:T(8,128)(2,1)} %partial_spectra.1), calls=%async_computation | async-start | bytes 524288 | tf_op jit(solution)/shard_map/all_to_all | solution.py:481
  9.2 0.7 %copy-start = (s32[2048,1]{0,1:T(1,128)S(1)}, s32[2048,1]{0,1:T(1,128)}, u32[]{:S(2)}) copy-start(s32[2048,1]{0,1:T(1,128)} %param.12) | copy-start | bytes 24580
  9.9 0.7 %copy-start.2 = (s32[2048]{0:T(1024)S(1)}, s32[2048]{0:T(1024)}, u32[]{:S(2)}) copy-start(s32[2048]{0:T(1024)} %param.13) | copy-start | bytes 24580
  10.6 3.6 %copy-start.1 = (s32[2048,1]{0,1:T(1,128)S(1)}, s32[2048,1]{0,1:T(1,128)}, u32[]{:S(2)}) copy-start(s32[2048,1]{0,1:T(1,128)} %param.12) | copy-start | bytes 24580
  10.6 3.6 %copy-start.3 = (s32[2048]{0:T(1024)S(1)}, s32[2048]{0:T(1024)}, u32[]{:S(2)}) copy-start(s32[2048]{0:T(1024)} %param.13) | copy-start | bytes 24580
  10.6 3.6 %copy-start.4 = (s32[2048]{0:T(1024)S(1)}, s32[2048]{0:T(1024)}, u32[]{:S(2)}) copy-start(s32[2048]{0:T(1024)} %param.14) | copy-start | bytes 24580
  15.5 20.9 %all-to-all-start.1 = ((bf16[32,16,128]{2,1,0:T(8,128)(2,1)}), bf16[32,16,128]{2,1,0:T(8,128)(2,1)S(1)}, u32[]{:S(2)}, u32[]{:S(2)}) async-start(bf16[32,16,128]{2,1,0:T(8,128)(2,1)} %place.1.sent_hbm), calls=%async_computation.1 | async-start | bytes 262144 | tf_op jit(solution)/shard_map/all_to_all | solution.py:484
  26.7 9.7 %copy-start.5 = (bf16[256,256]{1,0:T(8,128)(2,1)S(1)}, bf16[256,256]{1,0:T(8,128)(2,1)}, u32[]{:S(2)}) copy-start(bf16[256,256]{1,0:T(8,128)(2,1)} %constant.8.clone.tablet_hbm) | copy-start | bytes 393220
  26.7 9.7 %copy-start.6 = (bf16[256,256]{1,0:T(8,128)(2,1)S(1)}, bf16[256,256]{1,0:T(8,128)(2,1)}, u32[]{:S(2)}) copy-start(bf16[256,256]{1,0:T(8,128)(2,1)} %constant.7.clone.table_hbm) | copy-start | bytes 393220

commit v4 on v3

--- a/solution.py
+++ b/solution.py
@@ -26,7 +26,8 @@
 PARTS = 8
 SPAN = CAP // PARTS
 DEPTH = TILES * SPAN
-UNROLL = 16
+FIRST = 16
+MORE = 4
 PIECES = 1
 PIECE = ROWS // PIECES
 NT_DIMS = (((1,), (1,)), ((), ()))
@@ -205,8 +206,7 @@
     out_hbm,
     xa,
     xb,
-    ya,
-    yb,
+    y_all,
     parts,
     cells,
     acc,
@@ -250,14 +250,14 @@
     for cell in range(PARTS * CLASSES):
         cells[number] = cell
         number = number + (lax.shift_right_logical(mask, jnp.int32(cell)) & 1)
-    for extra in range(UNROLL + 1):
+    for extra in range(FIRST + 1):
         cells[number + extra] = PARTS * CLASSES
 
     iota = lax.broadcasted_iota(jnp.int32, (16, CAP), 0).astype(jnp.float32)
     one = jnp.ones((16, CAP), jnp.bfloat16)
     zero = jnp.zeros((16, CAP), jnp.bfloat16)
 
-    def build(x_buf, y_buf, cell):
+    def build(x_buf, cell):
         part = cell // CLASSES
         start = ((cell % CLASSES) * WIDE).astype(jnp.float32)
         for i in range(DEPTH // CAP):
@@ -265,33 +265,47 @@
             tail = parts[part, :, cut].astype(jnp.float32)
             rows = [
                 jnp.broadcast_to(tail[c : c + 1], (16, CAP)).astype(jnp.bfloat16)
-                for c in range(COLS + 2)
+                for c in range(COLS + 1)
             ]
             for r in range(WIDE // 16):
                 in_x = (iota + (start + 16.0 * r)).astype(jnp.bfloat16) == rows[COLS]
                 for c in range(COLS):
                     at = c * WIDE + r * 16
                     x_buf[at : at + 16, cut] = jnp.where(in_x, rows[c], zero)
+
+    def add(x_buf, cell):
+        acc[cell % CLASSES] += lax.dot_general(
+            x_buf[...], y_all[cell // CLASSES], NT_DIMS, preferred_element_type=jnp.float32
+        )
+
+    for e in range(PARTS):
+        for i in range(DEPTH // CAP):
+            cut = slice(i * CAP, (i + 1) * CAP)
+            tail = parts[e, :, cut].astype(jnp.float32)
+            row = jnp.broadcast_to(tail[COLS + 1 : COLS + 2], (16, CAP)).astype(jnp.bfloat16)
             for r in range(MIDS // 16):
-                in_y = (iota + 16.0 * r).astype(jnp.bfloat16) == rows[COLS + 1]
-                y_buf[r * 16 : (r + 1) * 16, cut] = jnp.where(in_y, one, zero)
-
-    def add(x_buf, y_buf, cell):
-        acc[cell % CLASSES] += lax.dot_general(
-            x_buf[...], y_buf[...], NT_DIMS, preferred_element_type=jnp.float32
-        )
-
+                in_y = (iota + 16.0 * r).astype(jnp.bfloat16) == row
+                y_all[e, r * 16 : (r + 1) * 16, cut] = jnp.where(in_y, one, zero)
+    y_all[PARTS] = jnp.zeros((MIDS, DEPTH), jnp.bfloat16)
     acc[...] = jnp.zeros_like(acc)
-    build(xa, ya, cells[0])
-
-    def many(p, _):
-        for k in range(UNROLL):
-            here, there = ((xa, ya), (xb, yb))[:: 1 if k % 2 == 0 else -1]
-            build(*there, cells[UNROLL * p + k + 1])
-            add(*here, cells[UNROLL * p + k])
+    build(xa, cells[0])
+
+    def work(first, count):
+        for k in range(count):
+            here, there = (xa, xb) if k % 2 == 0 else (xb, xa)
+            build(there, cells[first + k + 1])
+            add(here, cells[first + k])
+
+    def more(p, _):
+        work(FIRST + MORE * p, MORE)
         return 0
 
-    lax.fori_loop(0, (number + UNROLL - 1) // UNROLL, many, 0)
+    def most(p, _):
+        work(FIRST * p, FIRST)
+        return 0
+
+    lax.fori_loop(0, jnp.minimum(number, 1), most, 0)
+    lax.fori_loop(0, (jnp.maximum(number - FIRST, 0) + MORE - 1) // MORE, more, 0)
     for copy in copies:
         copy.wait()
 
@@ -455,10 +469,9 @@
         scratch_shapes=[
             pltpu.VMEM((COLS * WIDE, DEPTH), jnp.bfloat16),
             pltpu.VMEM((COLS * WIDE, DEPTH), jnp.bfloat16),
-            pltpu.VMEM((MIDS, DEPTH), jnp.bfloat16),
-            pltpu.VMEM((MIDS, DEPTH), jnp.bfloat16),
+            pltpu.VMEM((PARTS + 1, MIDS, DEPTH), jnp.bfloat16),
             pltpu.VMEM((PARTS + 1, 16, DEPTH), jnp.bfloat16),
-            pltpu.SMEM((PARTS * CLASSES + UNROLL + 2,), jnp.int32),
+            pltpu.SMEM((PARTS * CLASSES + FIRST + 2,), jnp.int32),
             pltpu.VMEM((CLASSES, COLS * WIDE, MIDS), jnp.float32),
             pltpu.VMEM((MIDS, MIDS), jnp.bfloat16),
             pltpu.VMEM((MIDS, MIDS), jnp.bfloat16),

time: 44.5 us -> 44.3 us (level)
  no operation moved by 1% of the time
where the time goes in v4:
time: 44.3 us; the launch traced here: 43.7 us
  starting transfers between devices  15.7 us (35%)
  Pallas kernels  13.1 us (30%)
  waiting for transfers between devices  10.9 us (25%)
  between operations  2.66 us (6%)
  local copies, waits for them, and re-layouts  1.41 us (3%)
    all_to_all x1, starting transfers between devices, per_device(): got = lax.all_to_all(sent, 'tile', split_axis=0, concat_axis=0, tiled=True)  11.2 us
    all_to_all x1, waiting for transfers between devices, per_device(): got = lax.all_to_all(sent, 'tile', split_axis=0, concat_axis=0, tiled=True)  7.92 us
    pallas_call x1, Pallas kernels, tile_image(): pl.pallas_call(tile_kernel, out_shape=jax.ShapeDtypeStruct((F_DEV, MIDS,...  7.3 us
    all_to_all x1, starting transfers between devices, per_device(): part = lax.all_to_all(part, 'band', split_axis=0, concat_axis=0, tiled=True)  4.47 us
    all_to_all x1, waiting for transfers between devices, per_device(): part = lax.all_to_all(part, 'band', split_axis=0, concat_axis=0, tiled=True)  2.96 us
    pallas_call x1, Pallas kernels, partial_spectra(): pl.pallas_call(partial_kernel, out_shape=jax.ShapeDtypeStruct((BANDS, 16,...  2.09 us
    pallas_call x1, Pallas kernels, phase_table(): pl.pallas_call(phase_kernel, out_shape=jax.ShapeDtypeStruct((2, F_DEV, MI...  1.73 us
    unnamed x14, local copies, waits for them, and re-layouts  1.41 us
  transfers between devices with their start and end apart: 2, of which 2 were waited for; matrix products, arithmetic and copies ran while one was open for 0% of the time, Pallas kernels for 5%

profile of v4, /device:TPU:32, one launch (start us, length us, event | category | flops | bytes accessed | tf_op | source)
XLA Modules:
  0.0 43.7 jit_solution(16014193904445025874)
XLA Ops:
  0.0 2.1 %partial_spectra.1 = bf16[8,16,1024]{2,1,0:T(8,128)(2,1)} custom-call(bf16[8,64,128]{2,1,0:T(8,128)(2,1)} %constant.6.clone.kern_hbm, bf16[2048,128]{1,0:T(8,128)(2,1)} %traces_hbm.1), custom_call_target="tpu_custom_call" | custom-call | flops 33554432 | bytes 800000 | tf_op jit(solution)/shard_map/partial_spectra/pallas_call | solution.py:403
  2.1 4.5 %all-to-all-start = ((bf16[8,16,1024]{2,1,0:T(8,128)(2,1)}), bf16[8,16,1024]{2,1,0:T(8,128)(2,1)S(1)}, u32[]{:S(2)}, u32[]{:S(2)}) async-start(bf16[8,16,1024]{2,1,0:T(8,128)(2,1)} %partial_spectra.1), calls=%async_computation | async-start | bytes 524288 | tf_op jit(solution)/shard_map/all_to_all | solution.py:494
  9.2 0.0 copy-start
  9.2 0.7 %copy-done = s32[2048,1]{0,1:T(1,128)S(1)} copy-done((s32[2048,1]{0,1:T(1,128)S(1)}, s32[2048,1]{0,1:T(1,128)}, u32[]{:S(2)}) %copy-start) | copy-done | bytes 8216
  9.9 0.0 copy-start.2
  9.9 0.7 %copy-done.2 = s32[2048]{0:T(1024)S(1)} copy-done((s32[2048]{0:T(1024)S(1)}, s32[2048]{0:T(1024)}, u32[]{:S(2)}) %copy-start.2) | copy-done | bytes 8216
  10.6 0.0 copy-start.1
  10.6 0.0 copy-start.3
  10.6 0.0 copy-start.4
  10.6 0.6 %slot_ranks.1 = (s32[1,2048]{1,0:T(1,128)S(1)}, s32[4,8,128]{2,1,0:T(8,128)S(1)}) custom-call(s32[1,2048]{1,0:T(1,128)S(1)} %bitcast.4, s32[1,2048]{1,0:T(1,128)S(1)} %bitcast.6, s32[1]{0:T(128)S(6)} %copy.12.low_ref, s32[1]{0:T(128)S(6)} %copy.13.high_ref, s32[1]{0:T(128)S(6)} %copy.14.offset_ref, s32[1]{0:T(128)S(6)} %copy.15.azimuth_ref), custom_call_target="tpu_custom_call" | custom-call | flops 2000000000 | bytes 3000000 | tf_op jit(solution)/shard_map/slot_ranks/pallas_call | solution.py:421
  11.2 3.0 %all-to-all-done.part_ref = bf16[8,16,1024]{2,1,0:T(8,128)(2,1)S(1)} async-done(((bf16[8,16,1024]{2,1,0:T(8,128)(2,1)}), bf16[8,16,1024]{2,1,0:T(8,128)(2,1)S(1)}, u32[]{:S(2)}, u32[]{:S(2)}) %all-to-all-start) | async-done | bytes 262176 | tf_op jit(solution)/shard_map/all_to_all | solution.py:494
  14.1 0.0 copy-done.1
  14.1 0.0 copy-done.3
  14.1 0.0 copy-done.4
  14.1 1.4 %place.1.sent_hbm = bf16[32,16,128]{2,1,0:T(8,128)(2,1)} custom-call(bf16[8,16,1024]{2,1,0:T(8,128)(2,1)S(1)} %all-to-all-done.part_ref, s32[1,2048]{1,0:T(1,128)S(1)} %get-tuple-element.7.rank_ref, s32[1,2048]{1,0:T(1,128)S(1)} %bitcast.5, s32[1,2048]{1,0:T(1,128)S(1)} %bitcast.7, s32[1,2048]{1,0:T(1,128)S(1)} %bitcast.8), custom_call_target="tpu_custom_call" | custom-call | flops 268435456 | bytes 1000000 | tf_op jit(solution)/shard_map/place/pallas_call | solution.py:449
  15.5 11.2 %all-to-all-start.1 = ((bf16[32,16,128]{2,1,0:T(8,128)(2,1)}), bf16[32,16,128]{2,1,0:T(8,128)(2,1)S(1)}, u32[]{:S(2)}, u32[]{:S(2)}) async-start(bf16[32,16,128]{2,1,0:T(8,128)(2,1)} %place.1.sent_hbm), calls=%async_computation.1 | async-start | bytes 262144 | tf_op jit(solution)/shard_map/all_to_all | solution.py:497
  26.7 0.0 copy-start.5
  26.7 0.0 copy-start.6
  26.7 1.7 %phase_table.1.phase_hbm = f32[2,4,256,256]{3,2,1,0:T(8,128)S(1)} custom-call(s32[4,8,128]{2,1,0:T(8,128)S(1)} %get-tuple-element.8.bins_ref, bf16[32,16,128]{2,1,0:T(8,128)(2,1)} %place.1.sent_hbm), custom_call_target="tpu_custom_call" | custom-call | flops 2000000000 | bytes 3000000 | tf_op jit(solution)/shard_map/phase_table/pallas_call | solution.py:437
  28.5 7.9 %all-to-all-done.1.got_ref = bf16[32,16,128]{2,1,0:T(8,128)(2,1)S(1)} async-done(((bf16[32,16,128]{2,1,0:T(8,128)(2,1)}), bf16[32,16,128]{2,1,0:T(8,128)(2,1)S(1)}, u32[]{:S(2)}, u32[]{:S(2)}) %all-to-all-start.1) | async-done | bytes 131104 | tf_op jit(solution)/shard_map/all_to_all | solution.py:497
  36.4 0.0 copy-done.5
  36.4 0.0 copy-done.6
  36.4 7.3 %tile_image.1 = f32[4,256,512]{2,1,0:T(8,128)} custom-call(bf16[32,16,128]{2,1,0:T(8,128)(2,1)S(1)} %all-to-all-done.1.got_ref, bf16[256,256]{1,0:T(8,128)(2,1)S(1)} %copy-done.6, bf16[256,256]{1,0:T(8,128)(2,1)S(1)} %copy-done.5, f32[2,4,256,256]{3,2,1,0:T(8,128)S(1)} %phase_table.1.phase_hbm), custom_call_target="tpu_custom_call" | custom-call | flops 6000000000 | bytes 5000000 | tf_op jit(solution)/shard_map/tile_image/pallas_call | solution.py:464
Async XLA Ops:
  2.1 12.0 %all-to-all-start = ((bf16[8,16,1024]{2,1,0:T(8,128)(2,1)}), bf16[8,16,1024]{2,1,0:T(8,128)(2,1)S(1)}, u32[]{:S(2)}, u32[]{:S(2)}) async-start(bf16[8,16,1024]{2,1,0:T(8,128)(2,1)} %partial_spectra.1), calls=%async_computation | async-start | bytes 524288 | tf_op jit(solution)/shard_map/all_to_all | solution.py:494
  9.2 0.7 %copy-start = (s32[2048,1]{0,1:T(1,128)S(1)}, s32[2048,1]{0,1:T(1,128)}, u32[]{:S(2)}) copy-start(s32[2048,1]{0,1:T(1,128)} %param.12) | copy-start | bytes 24580
  9.9 0.7 %copy-start.2 = (s32[2048]{0:T(1024)S(1)}, s32[2048]{0:T(1024)}, u32[]{:S(2)}) copy-start(s32[2048]{0:T(1024)} %param.13) | copy-start | bytes 24580
  10.6 3.6 %copy-start.1 = (s32[2048,1]{0,1:T(1,128)S(1)}, s32[2048,1]{0,1:T(1,128)}, u32[]{:S(2)}) copy-start(s32[2048,1]{0,1:T(1,128)} %param.12) | copy-start | bytes 24580
  10.6 3.6 %copy-start.3 = (s32[2048]{0:T(1024)S(1)}, s32[2048]{0:T(1024)}, u32[]{:S(2)}) copy-start(s32[2048]{0:T(1024)} %param.13) | copy-start | bytes 24580
  10.6 3.6 %copy-start.4 = (s32[2048]{0:T(1024)S(1)}, s32[2048]{0:T(1024)}, u32[]{:S(2)}) copy-start(s32[2048]{0:T(1024)} %param.14) | copy-start | bytes 24580
  15.5 20.9 %all-to-all-start.1 = ((bf16[32,16,128]{2,1,0:T(8,128)(2,1)}), bf16[32,16,128]{2,1,0:T(8,128)(2,1)S(1)}, u32[]{:S(2)}, u32[]{:S(2)}) async-start(bf16[32,16,128]{2,1,0:T(8,128)(2,1)} %place.1.sent_hbm), calls=%async_computation.1 | async-start | bytes 262144 | tf_op jit(solution)/shard_map/all_to_all | solution.py:497
  26.7 9.7 %copy-start.5 = (bf16[256,256]{1,0:T(8,128)(2,1)S(1)}, bf16[256,256]{1,0:T(8,128)(2,1)}, u32[]{:S(2)}) copy-start(bf16[256,256]{1,0:T(8,128)(2,1)} %constant.8.clone.tablet_hbm) | copy-start | bytes 393220
  26.7 9.7 %copy-start.6 = (bf16[256,256]{1,0:T(8,128)(2,1)S(1)}, bf16[256,256]{1,0:T(8,128)(2,1)}, u32[]{:S(2)}) copy-start(bf16[256,256]{1,0:T(8,128)(2,1)} %constant.7.clone.table_hbm) | copy-start | bytes 393220

commit v5 on v4

--- a/solution.py
+++ b/solution.py
@@ -173,7 +173,9 @@
             cos_f, sin_f = cos_f * turn_c - sin_f * turn_s, cos_f * turn_s + sin_f * turn_c
 
 
-def place_kernel(part_ref, rank_ref, route_ref, x_ref, y_ref, out_ref, masked):
+def place_kernel(
+    part_ref, rank_ref, route_ref, x_ref, y_ref, out_hbm, masked, placed, sems
+):
     row = lax.broadcasted_iota(jnp.int32, (8, ROWS), 0)
     mids = jnp.where(
         row == 0,
@@ -192,10 +194,25 @@
         [total[h * COLS : (h + 1) * COLS, cut] for cut in lanes for h in range(2)], axis=1
     )
     values = jnp.concatenate([spectra, mids], axis=0)
-    for g in range(TILES):
-        masked[g * 16 : (g + 1) * 16, :] = jnp.where(tile == g, values, 0.0).astype(jnp.bfloat16)
-    placed = lax.dot_general(masked[...], slots, NT_DIMS, preferred_element_type=jnp.float32)
-    out_ref[...] = placed.astype(jnp.bfloat16).reshape(TILES, 16, CAP)
+    some = TILES // 2
+    puts = []
+    for k in range(2):
+        for g in range(k * some, (k + 1) * some):
+            masked[g * 16 : (g + 1) * 16, :] = jnp.where(tile == g, values, 0.0).astype(
+                jnp.bfloat16
+            )
+        block = lax.dot_general(
+            masked[k * some * 16 : (k + 1) * some * 16, :],
+            slots,
+            NT_DIMS,
+            preferred_element_type=jnp.float32,
+        )
+        at = pl.ds(k * some, some)
+        placed[at] = block.astype(jnp.bfloat16).reshape(some, 16, CAP)
+        puts.append(pltpu.make_async_copy(placed.at[at], out_hbm.at[at], sems.at[k]))
+        puts[k].start()
+    for put in puts:
+        put.wait()
 
 
 def tile_kernel(
@@ -450,9 +467,11 @@
         place_kernel,
         out_shape=jax.ShapeDtypeStruct((TILES, 16, CAP), jnp.bfloat16),
         in_specs=[VM] * 5,
-        out_specs=VM,
+        out_specs=ANY,
         scratch_shapes=[
             pltpu.VMEM((TILES * 16, ROWS), jnp.bfloat16),
+            pltpu.VMEM((TILES, 16, CAP), jnp.bfloat16),
+            pltpu.SemaphoreType.DMA((2,)),
         ],
         compiler_params=vmem(16),
         cost_estimate=cost(2 * 512 * ROWS * CAP, 1_000_000),

time: 44.3 us -> 44.3 us (level)
  no operation moved by 1% of the time
where the time goes in v5:
time: 44.3 us; the launch traced here: 43.7 us
  starting transfers between devices  15.7 us (35%)
  Pallas kernels  13.1 us (30%)
  waiting for transfers between devices  10.9 us (25%)
  between operations  2.67 us (6%)
  local copies, waits for them, and re-layouts  1.41 us (3%)
    all_to_all x1, starting transfers between devices, per_device(): got = lax.all_to_all(sent, 'tile', split_axis=0, concat_axis=0, tiled=True)  11.2 us
    all_to_all x1, waiting for transfers between devices, per_device(): got = lax.all_to_all(sent, 'tile', split_axis=0, concat_axis=0, tiled=True)  7.92 us
    pallas_call x1, Pallas kernels, tile_image(): pl.pallas_call(tile_kernel, out_shape=jax.ShapeDtypeStruct((F_DEV, MIDS,...  7.31 us
    all_to_all x1, starting transfers between devices, per_device(): part = lax.all_to_all(part, 'band', split_axis=0, concat_axis=0, tiled=True)  4.47 us
    all_to_all x1, waiting for transfers between devices, per_device(): part = lax.all_to_all(part, 'band', split_axis=0, concat_axis=0, tiled=True)  2.96 us
    pallas_call x1, Pallas kernels, partial_spectra(): pl.pallas_call(partial_kernel, out_shape=jax.ShapeDtypeStruct((BANDS, 16,...  2.09 us
    pallas_call x1, Pallas kernels, phase_table(): pl.pallas_call(phase_kernel, out_shape=jax.ShapeDtypeStruct((2, F_DEV, MI...  1.73 us
    unnamed x14, local copies, waits for them, and re-layouts  1.41 us
  transfers between devices with their start and end apart: 2, of which 2 were waited for; matrix products, arithmetic and copies ran while one was open for 0% of the time, Pallas kernels for 5%

profile of v5, /device:TPU:32, one launch (start us, length us, event | category | flops | bytes accessed | tf_op | source)
XLA Modules:
  0.0 43.7 jit_solution(13239694689383100235)
XLA Ops:
  0.0 2.1 %partial_spectra.1 = bf16[8,16,1024]{2,1,0:T(8,128)(2,1)} custom-call(bf16[8,64,128]{2,1,0:T(8,128)(2,1)} %constant.6.clone.kern_hbm, bf16[2048,128]{1,0:T(8,128)(2,1)} %traces_hbm.1), custom_call_target="tpu_custom_call" | custom-call | flops 33554432 | bytes 800000 | tf_op jit(solution)/shard_map/partial_spectra/pallas_call | solution.py:420
  2.1 4.5 %all-to-all-start = ((bf16[8,16,1024]{2,1,0:T(8,128)(2,1)}), bf16[8,16,1024]{2,1,0:T(8,128)(2,1)S(1)}, u32[]{:S(2)}, u32[]{:S(2)}) async-start(bf16[8,16,1024]{2,1,0:T(8,128)(2,1)} %partial_spectra.1), calls=%async_computation | async-start | bytes 524288 | tf_op jit(solution)/shard_map/all_to_all | solution.py:513
  9.2 0.0 copy-start
  9.2 0.7 %copy-done = s32[2048,1]{0,1:T(1,128)S(1)} copy-done((s32[2048,1]{0,1:T(1,128)S(1)}, s32[2048,1]{0,1:T(1,128)}, u32[]{:S(2)}) %copy-start) | copy-done | bytes 8216
  9.9 0.0 copy-start.2
  9.9 0.7 %copy-done.2 = s32[2048]{0:T(1024)S(1)} copy-done((s32[2048]{0:T(1024)S(1)}, s32[2048]{0:T(1024)}, u32[]{:S(2)}) %copy-start.2) | copy-done | bytes 8216
  10.6 0.0 copy-start.1
  10.6 0.0 copy-start.3
  10.6 0.0 copy-start.4
  10.6 0.6 %slot_ranks.1 = (s32[1,2048]{1,0:T(1,128)S(1)}, s32[4,8,128]{2,1,0:T(8,128)S(1)}) custom-call(s32[1,2048]{1,0:T(1,128)S(1)} %bitcast.4, s32[1,2048]{1,0:T(1,128)S(1)} %bitcast.6, s32[1]{0:T(128)S(6)} %copy.12.low_ref, s32[1]{0:T(128)S(6)} %copy.13.high_ref, s32[1]{0:T(128)S(6)} %copy.14.offset_ref, s32[1]{0:T(128)S(6)} %copy.15.azimuth_ref), custom_call_target="tpu_custom_call" | custom-call | flops 2000000000 | bytes 3000000 | tf_op jit(solution)/shard_map/slot_ranks/pallas_call | solution.py:438
  11.2 3.0 %all-to-all-done.part_ref = bf16[8,16,1024]{2,1,0:T(8,128)(2,1)S(1)} async-done(((bf16[8,16,1024]{2,1,0:T(8,128)(2,1)}), bf16[8,16,1024]{2,1,0:T(8,128)(2,1)S(1)}, u32[]{:S(2)}, u32[]{:S(2)}) %all-to-all-start) | async-done | bytes 262176 | tf_op jit(solution)/shard_map/all_to_all | solution.py:513
  14.1 0.0 copy-done.1
  14.1 0.0 copy-done.3
  14.1 0.0 copy-done.4
  14.1 1.4 %place.1.sent_hbm = bf16[32,16,128]{2,1,0:T(8,128)(2,1)} custom-call(bf16[8,16,1024]{2,1,0:T(8,128)(2,1)S(1)} %all-to-all-done.part_ref, s32[1,2048]{1,0:T(1,128)S(1)} %get-tuple-element.7.rank_ref, s32[1,2048]{1,0:T(1,128)S(1)} %bitcast.5, s32[1,2048]{1,0:T(1,128)S(1)} %bitcast.7, s32[1,2048]{1,0:T(1,128)S(1)} %bitcast.8), custom_call_target="tpu_custom_call" | custom-call | flops 268435456 | bytes 1000000 | tf_op jit(solution)/shard_map/place/pallas_call | solution.py:466
  15.5 11.2 %all-to-all-start.1 = ((bf16[32,16,128]{2,1,0:T(8,128)(2,1)}), bf16[32,16,128]{2,1,0:T(8,128)(2,1)S(1)}, u32[]{:S(2)}, u32[]{:S(2)}) async-start(bf16[32,16,128]{2,1,0:T(8,128)(2,1)} %place.1.sent_hbm), calls=%async_computation.1 | async-start | bytes 262144 | tf_op jit(solution)/shard_map/all_to_all | solution.py:516
  26.7 0.0 copy-start.5
  26.7 0.0 copy-start.6
  26.7 1.7 %phase_table.1.phase_hbm = f32[2,4,256,256]{3,2,1,0:T(8,128)S(1)} custom-call(s32[4,8,128]{2,1,0:T(8,128)S(1)} %get-tuple-element.8.bins_ref, bf16[32,16,128]{2,1,0:T(8,128)(2,1)} %place.1.sent_hbm), custom_call_target="tpu_custom_call" | custom-call | flops 2000000000 | bytes 3000000 | tf_op jit(solution)/shard_map/phase_table/pallas_call | solution.py:454
  28.5 7.9 %all-to-all-done.1.got_ref = bf16[32,16,128]{2,1,0:T(8,128)(2,1)S(1)} async-done(((bf16[32,16,128]{2,1,0:T(8,128)(2,1)}), bf16[32,16,128]{2,1,0:T(8,128)(2,1)S(1)}, u32[]{:S(2)}, u32[]{:S(2)}) %all-to-all-start.1) | async-done | bytes 131104 | tf_op jit(solution)/shard_map/all_to_all | solution.py:516
  36.4 0.0 copy-done.5
  36.4 0.0 copy-done.6
  36.4 7.3 %tile_image.1 = f32[4,256,512]{2,1,0:T(8,128)} custom-call(bf16[32,16,128]{2,1,0:T(8,128)(2,1)S(1)} %all-to-all-done.1.got_ref, bf16[256,256]{1,0:T(8,128)(2,1)S(1)} %copy-done.6, bf16[256,256]{1,0:T(8,128)(2,1)S(1)} %copy-done.5, f32[2,4,256,256]{3,2,1,0:T(8,128)S(1)} %phase_table.1.phase_hbm), custom_call_target="tpu_custom_call" | custom-call | flops 6000000000 | bytes 5000000 | tf_op jit(solution)/shard_map/tile_image/pallas_call | solution.py:483
Async XLA Ops:
  2.1 12.0 %all-to-all-start = ((bf16[8,16,1024]{2,1,0:T(8,128)(2,1)}), bf16[8,16,1024]{2,1,0:T(8,128)(2,1)S(1)}, u32[]{:S(2)}, u32[]{:S(2)}) async-start(bf16[8,16,1024]{2,1,0:T(8,128)(2,1)} %partial_spectra.1), calls=%async_computation | async-start | bytes 524288 | tf_op jit(solution)/shard_map/all_to_all | solution.py:513
  9.2 0.7 %copy-start = (s32[2048,1]{0,1:T(1,128)S(1)}, s32[2048,1]{0,1:T(1,128)}, u32[]{:S(2)}) copy-start(s32[2048,1]{0,1:T(1,128)} %param.12) | copy-start | bytes 24580
  9.9 0.7 %copy-start.2 = (s32[2048]{0:T(1024)S(1)}, s32[2048]{0:T(1024)}, u32[]{:S(2)}) copy-start(s32[2048]{0:T(1024)} %param.13) | copy-start | bytes 24580
  10.6 3.6 %copy-start.1 = (s32[2048,1]{0,1:T(1,128)S(1)}, s32[2048,1]{0,1:T(1,128)}, u32[]{:S(2)}) copy-start(s32[2048,1]{0,1:T(1,128)} %param.12) | copy-start | bytes 24580
  10.6 3.6 %copy-start.3 = (s32[2048]{0:T(1024)S(1)}, s32[2048]{0:T(1024)}, u32[]{:S(2)}) copy-start(s32[2048]{0:T(1024)} %param.13) | copy-start | bytes 24580
  10.6 3.6 %copy-start.4 = (s32[2048]{0:T(1024)S(1)}, s32[2048]{0:T(1024)}, u32[]{:S(2)}) copy-start(s32[2048]{0:T(1024)} %param.14) | copy-start | bytes 24580
  15.5 20.9 %all-to-all-start.1 = ((bf16[32,16,128]{2,1,0:T(8,128)(2,1)}), bf16[32,16,128]{2,1,0:T(8,128)(2,1)S(1)}, u32[]{:S(2)}, u32[]{:S(2)}) async-start(bf16[32,16,128]{2,1,0:T(8,128)(2,1)} %place.1.sent_hbm), calls=%async_computation.1 | async-start | bytes 262144 | tf_op jit(solution)/shard_map/all_to_all | solution.py:516
  26.7 9.7 %copy-start.5 = (bf16[256,256]{1,0:T(8,128)(2,1)S(1)}, bf16[256,256]{1,0:T(8,128)(2,1)}, u32[]{:S(2)}) copy-start(bf16[256,256]{1,0:T(8,128)(2,1)} %constant.8.clone.tablet_hbm) | copy-start | bytes 393220
  26.7 9.7 %copy-start.6 = (bf16[256,256]{1,0:T(8,128)(2,1)S(1)}, bf16[256,256]{1,0:T(8,128)(2,1)}, u32[]{:S(2)}) copy-start(bf16[256,256]{1,0:T(8,128)(2,1)} %constant.7.clone.table_hbm) | copy-start | bytes 393220
